TPU v7x, 32 devices: a whole 2x2x4 slice. The times are simulated.
32 devices in a mesh: dp: 8 (over z, x), tensor: 4 (over y, core).
Axes of the slice: x: 2, y: 2, z: 4, core: 2. Of those that a mesh axis runs over, the one named last changes fastest.
Arguments:
- inputs: bfloat16 [16384, 1024], P('dp'), may hold values from -6 to 6
- w_qkv: bfloat16 [3, 1024, 1024], P(None, None, 'tensor'), may hold values from -0.1875 to 0.1875
- w_out: bfloat16 [1024, 1024], P('tensor'), may hold values from -0.1875 to 0.1875
- w_up: bfloat16 [1024, 4096], P(None, 'tensor'), may hold values from -0.1875 to 0.1875
- w_down: bfloat16 [4096, 1024], P('tensor'), may hold values from -0.09375 to 0.09375
- norm_gains: float32 [4, 1024], replicated, may hold values from 0.5 to 1.5
- norm_biases: float32 [4, 1024], replicated, may hold values from -1.5 to 1.5
- out_cot: bfloat16 [16384, 1024], P('dp'), may hold values from -6 to 6
- group_ids: int32 [16384], P('dp'), may hold values from 0 to 15
- group_weights: float32 [16], replicated, may hold values from 0.25 to 4
Outputs:
- layer_out: bfloat16 [16384, 1024], P(('dp', 'tensor'))
- input_grad: float32 [16384, 1024], P(('dp', 'tensor'))
- w_qkv_grad: float32 [3, 1024, 1024], P(None, 'dp', 'tensor')
- w_out_grad: float32 [1024, 1024], P('tensor', 'dp')
- w_up_grad: float32 [1024, 4096], P('dp', 'tensor')
- w_down_grad: float32 [4096, 1024], P('tensor', 'dp')
- gains_grad: float32 [4, 1024], P(None, ('dp', 'tensor'))
- biases_grad: float32 [4, 1024], P(None, ('dp', 'tensor'))
Inputs may be any that keep to these rules, and one draw needn't show every extreme that they name: `group_ids`: each token's index into group_weights.
All inputs are finite; a program needn't handle non-finite values.
Results may differ from a plain program's by a relative error of at most 0.013.
Values may be sent and summed in bfloat16 or wider, within the bound.
No kernel may reach another device: no remote copies, remote signals or barrier semaphores. Data moves between devices by JAX's collectives and lax.ppermute only.
A program may use at most 192 MiB of HBM per device.

v0:
```python
import math

import jax
import jax.numpy as jnp
from jax import lax
from jax.sharding import PartitionSpec as P

DH = 64
SEQ = 2048


EPS = 1e-05


def normalize(field_in):
    row_mean = jnp.mean(field_in, axis=-1, keepdims=True)
    centred = field_in - row_mean
    variance = jnp.mean(centred * centred, axis=-1, keepdims=True)
    inverse = lax.rsqrt(variance + EPS)
    return (centred * inverse, inverse)


def norm_back(grad_in, unit_rows, inverse, norm_gain):
    scaled = grad_in * norm_gain
    mean_one = jnp.mean(scaled, axis=-1, keepdims=True)
    mean_two = jnp.mean(scaled * unit_rows, axis=-1, keepdims=True)
    return inverse * (scaled - mean_one - unit_rows * mean_two)


def rotary_tables(length, head_size):
    half_size = head_size // 2
    frequency = jnp.exp(jnp.arange(half_size, dtype=jnp.float32) * (-math.log(10000.0) / half_size))
    angles = jnp.arange(length, dtype=jnp.float32)[:, None] * frequency[None, :]
    return (jnp.cos(angles)[:, None, :], jnp.sin(angles)[:, None, :])


def rotate(field_in, angle_cos, angle_sin):
    half_size = field_in.shape[-1] // 2
    first_half = field_in[..., :half_size]
    second_half = field_in[..., half_size:]
    return jnp.concatenate(
        [
            first_half * angle_cos - second_half * angle_sin,
            second_half * angle_cos + first_half * angle_sin,
        ],
        axis=-1,
    )


def rotate_back(grad_in, angle_cos, angle_sin):
    half_size = grad_in.shape[-1] // 2
    upper_half = grad_in[..., :half_size]
    lower_half = grad_in[..., half_size:]
    return jnp.concatenate(
        [
            upper_half * angle_cos + lower_half * angle_sin,
            lower_half * angle_cos - upper_half * angle_sin,
        ],
        axis=-1,
    )


def block_scores(query_block, key_seq, row_start, score_scale):
    length = key_seq.shape[0]
    block_rows = query_block.shape[0]
    scores = (
        jnp.einsum("qhd,khd->hqk", query_block, key_seq, preferred_element_type=jnp.float32)
        * score_scale
    )
    key_pos = jnp.arange(length, dtype=jnp.int32)
    query_pos = row_start + jnp.arange(block_rows, dtype=jnp.int32)
    allowed = key_pos[None, None, :] <= query_pos[None, :, None]
    return jnp.where(allowed, scores, -1e30)


def attend_forward(query_seq, key_seq, value_seq):
    length, head_count, head_size = query_seq.shape
    block_rows = min(512, length)
    blocks = length // block_rows
    score_scale = 1.0 / math.sqrt(head_size)

    def one_block(carried, block_index):
        row_start = block_index * block_rows
        query_block = lax.dynamic_slice_in_dim(query_seq, row_start, block_rows, 0)
        scores = block_scores(query_block, key_seq, row_start, score_scale)
        row_max = jnp.max(scores, axis=-1, keepdims=True)
        exp_scores = jnp.exp(scores - row_max)
        summed = jnp.sum(exp_scores, axis=-1, keepdims=True)
        chance_low = (exp_scores / summed).astype(jnp.bfloat16)
        result = jnp.einsum(
            "hqk,khd->qhd", chance_low, value_seq, preferred_element_type=jnp.float32
        )
        log_total = (row_max + jnp.log(summed))[..., 0]
        return (carried, (result.astype(jnp.bfloat16), log_total))

    unused, (results, log_totals) = lax.scan(
        one_block, jnp.int32(0), jnp.arange(blocks, dtype=jnp.int32)
    )
    return (results.reshape(length, head_count, head_size), log_totals)


def attend_backward(query_seq, key_seq, value_seq, log_totals, grad_seq):
    length, head_count, head_size = query_seq.shape
    block_rows = min(512, length)
    blocks = length // block_rows
    score_scale = 1.0 / math.sqrt(head_size)

    def one_block(carried, block_index):
        key_grad, value_grad = carried
        row_start = block_index * block_rows
        query_block = lax.dynamic_slice_in_dim(query_seq, row_start, block_rows, 0)
        grad_block = lax.dynamic_slice_in_dim(grad_seq, row_start, block_rows, 0)
        scores = block_scores(query_block, key_seq, row_start, score_scale)
        chance = jnp.exp(scores - log_totals[block_index][:, :, None])
        chance_low = chance.astype(jnp.bfloat16)
        chance_grad = jnp.einsum(
            "qhd,khd->hqk", grad_block, value_seq, preferred_element_type=jnp.float32
        )
        inner_sum = jnp.sum(chance * chance_grad, axis=-1, keepdims=True)
        score_grad = (chance * (chance_grad - inner_sum)).astype(jnp.bfloat16)
        query_grad = (
            jnp.einsum("hqk,khd->qhd", score_grad, key_seq, preferred_element_type=jnp.float32)
            * score_scale
        )
        key_grad = (
            key_grad
            + jnp.einsum(
                "hqk,qhd->khd", score_grad, query_block, preferred_element_type=jnp.float32
            )
            * score_scale
        )
        value_grad = value_grad + jnp.einsum(
            "hqk,qhd->khd", chance_low, grad_block, preferred_element_type=jnp.float32
        )
        return ((key_grad, value_grad), query_grad)

    zeros_seq = jnp.zeros((length, head_count, head_size), jnp.float32)
    (key_grad, value_grad), query_grads = lax.scan(
        one_block, (zeros_seq, zeros_seq), jnp.arange(blocks, dtype=jnp.int32)
    )
    return (query_grads.reshape(length, head_count, head_size), key_grad, value_grad)


def gelu_tanh(field_in):
    return jax.nn.gelu(field_in, approximate=True)


def forward_one(triple):
    return attend_forward(triple[0], triple[1], triple[2])


def backward_one(group_in):
    return attend_backward(group_in[0], group_in[1], group_in[2], group_in[3], group_in[4])


def per_device(
    inputs, w_qkv, w_out, w_up, w_down, norm_gains, norm_biases, out_cot, group_ids, group_weights
):
    tok_rows = inputs.shape[0]
    local_width = w_out.shape[0]
    head_count = local_width // DH
    sequences = tok_rows // SEQ
    share_rows = tok_rows // lax.axis_size("tensor")
    row_start = lax.axis_index("tensor") * share_rows
    angle_cos, angle_sin = rotary_tables(SEQ, DH)

    def take_rows(field_in):
        return lax.dynamic_slice_in_dim(field_in, row_start, share_rows, 0)

    def per_token(field_in):
        return field_in.reshape(sequences, SEQ, head_count, DH)

    def branch_out(partial_value, residual, norm_index):
        summed = lax.psum_scatter(partial_value, "tensor", scatter_dimension=0, tiled=True)
        residual = take_rows(residual)
        unit_rows, inverse = normalize(summed)
        return (
            residual + unit_rows * norm_gains[norm_index] + norm_biases[norm_index],
            unit_rows,
            inverse,
        )

    first_in = inputs.astype(jnp.float32)
    unit_in, inverse_in = normalize(first_in)
    normed = (unit_in * norm_gains[0] + norm_biases[0]).astype(jnp.bfloat16)
    projected = jnp.einsum("sd,cde->cse", normed, w_qkv, preferred_element_type=jnp.float32)
    query_all = rotate(per_token(projected[0]), angle_cos, angle_sin).astype(jnp.bfloat16)
    key_all = rotate(per_token(projected[1]), angle_cos, angle_sin).astype(jnp.bfloat16)
    value_all = per_token(projected[2].astype(jnp.bfloat16))
    attended, log_totals = lax.map(forward_one, (query_all, key_all, value_all))
    attended = attended.reshape(tok_rows, local_width)
    partial_attn = jnp.dot(attended, w_out, preferred_element_type=jnp.float32)
    state_rows, attn_unit, attn_inverse = branch_out(partial_attn, first_in, 1)
    middle = lax.all_gather(state_rows, "tensor", axis=0, tiled=True)
    mid_unit, mid_inverse = normalize(middle)
    mid_normed = (mid_unit * norm_gains[2] + norm_biases[2]).astype(jnp.bfloat16)
    hidden_in = jnp.dot(mid_normed, w_up, preferred_element_type=jnp.float32)
    activated = gelu_tanh(hidden_in).astype(jnp.bfloat16)
    partial_mlp = jnp.dot(activated, w_down, preferred_element_type=jnp.float32)
    final_rows, mlp_unit, mlp_inverse = branch_out(partial_mlp, middle, 3)
    lookup = (
        group_ids[:, None] == jnp.arange(group_weights.shape[0], dtype=jnp.int32)[None, :]
    ).astype(jnp.float32)
    row_weight = jnp.sum(lookup * group_weights[None, :], axis=1)
    grad_out = out_cot.astype(jnp.float32) * row_weight[:, None]
    grad_out_rows = take_rows(grad_out)
    mlp_branch_rows = norm_back(grad_out_rows, mlp_unit, mlp_inverse, norm_gains[3]).astype(
        jnp.bfloat16
    )
    mlp_branch = lax.all_gather(mlp_branch_rows, "tensor", axis=0, tiled=True)
    gain_three = jnp.sum(grad_out_rows * mlp_unit, axis=0)
    bias_three = jnp.sum(grad_out_rows, axis=0)
    down_grad = jnp.einsum("sf,sd->fd", activated, mlp_branch, preferred_element_type=jnp.float32)
    act_grad = jnp.einsum("sd,fd->sf", mlp_branch, w_down, preferred_element_type=jnp.float32)
    unused, gelu_pullback = jax.vjp(gelu_tanh, hidden_in)
    hidden_grad = gelu_pullback(act_grad)[0].astype(jnp.bfloat16)
    up_grad = jnp.einsum("sd,sf->df", mid_normed, hidden_grad, preferred_element_type=jnp.float32)
    mid_partial = jnp.einsum("sf,df->sd", hidden_grad, w_up, preferred_element_type=jnp.float32)
    mid_grad_rows = lax.psum_scatter(mid_partial, "tensor", scatter_dimension=0, tiled=True)
    mid_unit_rows = take_rows(mid_unit)
    state_grad = grad_out_rows + norm_back(
        mid_grad_rows, mid_unit_rows, take_rows(mid_inverse), norm_gains[2]
    )
    gain_two = jnp.sum(mid_grad_rows * mid_unit_rows, axis=0)
    bias_two = jnp.sum(mid_grad_rows, axis=0)
    branch_rows = norm_back(state_grad, attn_unit, attn_inverse, norm_gains[1]).astype(jnp.bfloat16)
    gain_one = jnp.sum(state_grad * attn_unit, axis=0)
    bias_one = jnp.sum(state_grad, axis=0)
    attn_branch = lax.all_gather(branch_rows, "tensor", axis=0, tiled=True)
    out_weight_grad = jnp.einsum(
        "se,sd->ed", attended, attn_branch, preferred_element_type=jnp.float32
    )
    attended_grad = jnp.einsum(
        "sd,ed->se", attn_branch, w_out, preferred_element_type=jnp.float32
    ).astype(jnp.bfloat16)
    query_grad, key_grad, value_grad = lax.map(
        backward_one, (query_all, key_all, value_all, log_totals, per_token(attended_grad))
    )
    proj_grad = jnp.stack(
        [
            rotate_back(query_grad, angle_cos, angle_sin).reshape(tok_rows, local_width),
            rotate_back(key_grad, angle_cos, angle_sin).reshape(tok_rows, local_width),
            value_grad.reshape(tok_rows, local_width),
        ]
    ).astype(jnp.bfloat16)
    qkv_grad = jnp.einsum("sd,cse->cde", normed, proj_grad, preferred_element_type=jnp.float32)
    in_partial = jnp.einsum("cse,cde->sd", proj_grad, w_qkv, preferred_element_type=jnp.float32)
    in_grad_rows = lax.psum_scatter(
        in_partial.astype(jnp.bfloat16), "tensor", scatter_dimension=0, tiled=True
    ).astype(jnp.float32)
    unit_in_rows = take_rows(unit_in)
    input_grad = state_grad + norm_back(
        in_grad_rows, unit_in_rows, take_rows(inverse_in), norm_gains[0]
    )
    gain_zero = jnp.sum(in_grad_rows * unit_in_rows, axis=0)
    bias_zero = jnp.sum(in_grad_rows, axis=0)
    qkv_total, out_total, up_total, down_total = (
        lax.psum_scatter(qkv_grad, "dp", scatter_dimension=1, tiled=True),
        lax.psum_scatter(out_weight_grad, "dp", scatter_dimension=1, tiled=True),
        lax.psum_scatter(up_grad, "dp", scatter_dimension=0, tiled=True),
        lax.psum_scatter(down_grad, "dp", scatter_dimension=1, tiled=True),
    )
    gain_parts = jnp.stack([gain_zero, gain_one, gain_two, gain_three])
    bias_parts = jnp.stack([bias_zero, bias_one, bias_two, bias_three])
    gains_grad, biases_grad = (
        lax.psum_scatter(gain_parts, ("dp", "tensor"), scatter_dimension=1, tiled=True),
        lax.psum_scatter(bias_parts, ("dp", "tensor"), scatter_dimension=1, tiled=True),
    )
    return (
        final_rows.astype(jnp.bfloat16),
        input_grad,
        qkv_total,
        out_total,
        up_total,
        down_total,
        gains_grad,
        biases_grad,
    )


def solution(mesh):
    placed = (
        P("dp", None),
        P(None, None, "tensor"),
        P("tensor", None),
        P(None, "tensor"),
        P("tensor", None),
        P(),
        P(),
        P("dp", None),
        P("dp"),
        P(),
    )
    return jax.shard_map(
        per_device,
        mesh=mesh,
        in_specs=placed,
        out_specs=(
            P(("dp", "tensor"), None),
            P(("dp", "tensor"), None),
            P(None, "dp", "tensor"),
            P("tensor", "dp"),
            P("dp", "tensor"),
            P("tensor", "dp"),
            P(None, ("dp", "tensor")),
            P(None, ("dp", "tensor")),
        ),
        check_vma=False,
    )
```

profile of v0, /device:TPU:0, one launch (start us, length us, event | category | flops | bytes accessed | tf_op | source)
XLA Modules:
  0.0 1438.8 jit_solution(8544679518114210716)
XLA Ops:
  26.7 69.5 %while.47 = (s32[]{:T(128)}, bf16[4,512,4,64]{1,3,2,0:T(8,128)(2,1)}, f32[4,4,512]{2,1,0:T(4,128)}, s32[4]{0:T(128)S(1)}, bf16[2048,4,64]{0,2,1:T(8,128)(2,1)}, ...) while((s32[]{:T(128)}, ...), condition=%wide.region_5.6_spmd, body=%wide.region_2.5_spmd.sunk | while | flops 1125251584 | bytes 61411544 | solution.py:96
  37.5 5.9 fusion.120
  54.8 5.9 fusion.120
  72.2 5.9 fusion.120
  89.5 5.9 fusion.120
  104.2 6.5 convert_element_type.66
  110.7 68.0 %reduce-scatter.15.cloned.1.call-done = f32[512,1024]{1,0:T(8,128)} async-done(((f32[2048,1024]{1,0:T(8,128)}), f32[512,1024]{1,0:T(8,128)}) %reduce-scatter.15.cloned.1.call-update) | async-done | bytes 2097168 | tf_op jit(solution)/shard_map/reduce_scatter | solution.py:174
  186.5 58.4 %all-gather.4.cloned.1.call-done = f32[2048,1024]{1,0:T(8,128)} async-done(((f32[512,1024]{1,0:T(8,128)}), f32[2048,1024]{1,0:T(8,128)}) %all-gather.4.cloned.1.call-update) | async-done | bytes 8388624 | tf_op jit(solution)/shard_map/all_gather | solution.py:194
  264.0 7.2 fusion.68
  272.1 71.0 %reduce-scatter.17.cloned.1.call-done = f32[512,1024]{1,0:T(8,128)} async-done(((f32[2048,1024]{1,0:T(8,128)}), f32[512,1024]{1,0:T(8,128)}) %reduce-scatter.17.cloned.1.call-update) | async-done | bytes 2097168 | tf_op jit(solution)/shard_map/reduce_scatter | solution.py:174
  354.0 34.6 %all-gather.6.cloned.1.call-done = bf16[2048,1024]{1,0:T(8,128)(2,1)} async-done(((bf16[512,1024]{1,0:T(8,128)(2,1)}), bf16[2048,1024]{1,0:T(8,128)(2,1)}) %all-gather.6.cloned.1.call-update) | async-done | bytes 4194320 | tf_op jit(solution)/shard_map/all_gather | solution.py:210
  388.6 12.2 fusion.42
  402.8 6.9 fusion.73
  409.9 71.7 %reduce-scatter.19.cloned.1.call-done = f32[512,1024]{1,0:T(8,128)} async-done(((f32[2048,1024]{1,0:T(8,128)}), f32[512,1024]{1,0:T(8,128)}) %reduce-scatter.19.cloned.1.call-update) | async-done | bytes 2097168 | tf_op jit(solution)/shard_map/reduce_scatter | solution.py:219
  492.3 34.6 %all-gather.8.cloned.1.call-done = bf16[2048,1024]{1,0:T(8,128)(2,1)} async-done(((bf16[512,1024]{1,0:T(8,128)(2,1)}), bf16[2048,1024]{1,0:T(8,128)(2,1)}) %all-gather.8.cloned.1.call-update) | async-done | bytes 4194320 | tf_op jit(solution)/shard_map/all_gather | solution.py:229
  531.5 241.8 %while.48 = (s32[]{:T(128)}, f32[2048,4,64]{0,2,1:T(8,128)}, f32[2048,4,64]{0,2,1:T(8,128)}, f32[4,512,4,64]{1,0,3,2:T(4,128)}, s32[4]{0:T(128)S(1)}, /*index=5*...) while((s32[]{:T(128)}, f32[2048,4,64]{0,2,1:T(8,128)}, ...), condition=%wide.region_24.25_spmd.clone, body=%wide.region_22.24_spmd.clone.sunk | while | flops 2751068672 | bytes 183038288 | solution.py:138
  539.8 7.2 fusion.132
  547.0 11.5 multiply_reduce_fusion.14
  558.5 10.9 multiply_convert_fusion.7
  569.4 6.2 fusion.133
  580.1 11.1 dynamic_update_slice.33
  599.3 7.6 fusion.132
  606.9 11.5 multiply_reduce_fusion.14
  618.4 10.9 multiply_convert_fusion.7
  629.3 6.2 fusion.133
  640.7 11.1 dynamic_update_slice.33
  659.9 7.6 fusion.132
  667.5 11.5 multiply_reduce_fusion.14
  679.1 10.9 multiply_convert_fusion.7
  690.0 6.2 fusion.133
  701.4 11.1 dynamic_update_slice.33
  720.6 7.6 fusion.132
  728.2 11.5 multiply_reduce_fusion.14
  739.7 10.9 multiply_convert_fusion.7
  750.6 6.2 fusion.133
  762.0 11.1 dynamic_update_slice.33
  785.7 7.5 bitcast_convert_fusion
  794.4 8.3 convolution_bitcast_fusion.1
  802.7 5.4 subtract_multiply_fusion.1
  808.2 29.7 %reduce-scatter.21.cloned.1.call-done = bf16[512,1024]{1,0:T(8,128)(2,1)} async-done(((bf16[2048,1024]{1,0:T(8,128)(2,1)}), bf16[512,1024]{1,0:T(8,128)(2,1)}) %reduce-scatter.21.cloned.1.call-update) | async-done | bytes 1048592 | tf_op jit(solution)/shard_map/reduce_scatter | solution.py:248
  843.1 12.0 fusion.67
  855.8 11.2 fusion.55
  872.8 43.8 %reduce-scatter.23.cloned.1.call-done = f32[3,128,256]{1,2,0:T(8,128)} async-done(((f32[3,1024,256]{1,2,0:T(8,128)}), f32[3,128,256]{1,2,0:T(8,128)}) %reduce-scatter.23.cloned.1.call-update) | async-done | bytes 393232 | tf_op jit(solution)/shard_map/reduce_scatter | solution.py:258
  922.6 129.3 %reduce-scatter.33.cloned.1.call-done = f32[32,4]{1,0:T(8,128)} async-done(((f32[1024,4]{1,0:T(8,128)}), f32[32,4]{1,0:T(8,128)}) %reduce-scatter.33.cloned.1.call-update) | async-done | bytes 528
  1053.2 130.4 %reduce-scatter.31.cloned.1.call-done = f32[32,4]{1,0:T(8,128)} async-done(((f32[1024,4]{1,0:T(8,128)}), f32[32,4]{1,0:T(8,128)}) %reduce-scatter.31.cloned.1.call-update) | async-done | bytes 528
  1185.0 87.1 %reduce-scatter.29.cloned.1.call-done = f32[1024,128]{1,0:T(8,128)} async-done(((f32[1024,1024]{1,0:T(8,128)}), f32[1024,128]{1,0:T(8,128)}) %reduce-scatter.29.cloned.1.call-update) | async-done | bytes 524304 | tf_op jit(solution)/shard_map/reduce_scatter | solution.py:261
  1272.0 92.2 %reduce-scatter.27.cloned.1.call-done = f32[128,1024]{1,0:T(8,128)} async-done(((f32[1024,1024]{1,0:T(8,128)}), f32[128,1024]{1,0:T(8,128)}) %reduce-scatter.27.cloned.1.call-update) | async-done | bytes 524304 | tf_op jit(solution)/shard_map/reduce_scatter | solution.py:260
  1364.2 67.6 %reduce-scatter.25.cloned.1.call-done = f32[256,128]{1,0:T(8,128)} async-done(((f32[256,1024]{1,0:T(8,128)}), f32[256,128]{1,0:T(8,128)}) %reduce-scatter.25.cloned.1.call-update) | async-done | bytes 131088 | tf_op jit(solution)/shard_map/reduce_scatter | solution.py:259
  (278 shorter events, 201.6 us)
Async XLA Ops:
  7.2 256.8 %copy-start = (bf16[1024,1024]{1,0:T(8,128)(2,1)S(1)}, bf16[1024,1024]{1,0:T(8,128)(2,1)}, u32[]{:S(2)}) copy-start(bf16[1024,1024]{1,0:T(8,128)(2,1)} %param.18) | copy-start | bytes 6291460
  7.2 171.5 %reduce-scatter.15.cloned.1.call-start = ((), (), s32[]{:S(2)}) async-start(), calls=%async_computation.10 | async-start | bytes 10485760 | tf_op jit(solution)/shard_map/reduce_scatter | solution.py:174
  7.3 5.0 copy-start.38
  7.3 5.6 copy-start.39
  7.3 6.2 copy-start.51
  10.8 7.0 copy-start.23
  12.3 5.6 copy-start.26
  12.9 4.9 copy-start.28
  13.5 4.3 copy-start.46
  22.5 4.2 copy-start.16
  22.5 4.2 copy-start.18
  33.1 4.3 copy-start.8
  50.5 4.3 copy-start.8
  67.8 4.3 copy-start.8
  85.1 4.3 copy-start.8
  104.2 140.8 %all-gather.4.cloned.1.call-start = ((), (), s32[]{:S(2)}) async-start(), calls=%async_computation.11 | async-start | bytes 10485760 | tf_op jit(solution)/shard_map/all_gather | solution.py:194
  110.7 71.8 %copy-start.25 = (f32[1,1024]{1,0:T(1,128)S(1)}, f32[1,1024]{1,0:T(1,128)}, u32[]{:S(2)}) copy-start(f32[1,1024]{1,0:T(1,128)} %get-tuple-element.287) | copy-start | bytes 12292
  110.7 71.8 %copy-start.42 = (f32[1,1024]{1,0:T(1,128)S(1)}, f32[1,1024]{1,0:T(1,128)}, u32[]{:S(2)}) copy-start(f32[1,1024]{1,0:T(1,128)} %get-tuple-element.291) | copy-start | bytes 12292
  186.5 156.6 %reduce-scatter.17.cloned.1.call-start = ((), (), s32[]{:S(2)}) async-start(), calls=%async_computation.12 | async-start | bytes 10485760 | tf_op jit(solution)/shard_map/reduce_scatter | solution.py:174
  248.8 5.8 copy-start.4
  255.5 5.2 copy-start.11
  271.2 75.7 %copy-start.30 = (f32[1,1024]{1,0:T(1,128)S(1)}, f32[1,1024]{1,0:T(1,128)}, u32[]{:S(2)}) copy-start(f32[1,1024]{1,0:T(1,128)} %get-tuple-element.286) | copy-start | bytes 12292
  271.2 79.2 %copy-start.37 = (f32[1,1024]{1,0:T(1,128)S(1)}, f32[1,1024]{1,0:T(1,128)}, u32[]{:S(2)}) copy-start(f32[1,1024]{1,0:T(1,128)} %get-tuple-element.290) | copy-start | bytes 12292
  271.2 117.4 %all-gather.6.cloned.1.call-start = ((), (), s32[]{:S(2)}) async-start(), calls=%async_computation.13 | async-start | bytes 5242880 | tf_op jit(solution)/shard_map/all_gather | solution.py:210
  344.9 5.6 copy-start.9
  354.0 127.6 %reduce-scatter.19.cloned.1.call-start = ((), (), s32[]{:S(2)}) async-start(), calls=%async_computation.14 | async-start | bytes 10485760 | tf_op jit(solution)/shard_map/reduce_scatter | solution.py:219
  388.6 14.1 copy-start.50
  409.7 75.5 %copy-start.7 = (f32[512,1024]{1,0:T(8,128)S(1)}, f32[512,1024]{1,0:T(8,128)}, u32[]{:S(2)}) copy-start(f32[512,1024]{1,0:T(8,128)} %reduce-scatter.15.cloned.1.call-done) | copy-start | bytes 6291460
  409.7 117.2 %all-gather.8.cloned.1.call-start = ((), (), s32[]{:S(2)}) async-start(), calls=%async_computation.15 | async-start | bytes 5242880 | tf_op jit(solution)/shard_map/all_gather | solution.py:229
  492.2 345.6 %reduce-scatter.21.cloned.1.call-start = ((), (), s32[]{:S(2)}) async-start(), calls=%async_computation.16 | async-start | bytes 5242880 | tf_op jit(solution)/shard_map/reduce_scatter | solution.py:248
  569.4 6.2 copy-start.2
  629.3 6.2 copy-start.2
  690.0 6.2 copy-start.2
  750.6 6.2 copy-start.2
  793.2 123.4 %reduce-scatter.23.cloned.1.call-start = ((), (), s32[]{:S(2)}) async-start(), calls=%async_computation.17 | async-start | bytes 3538944 | tf_op jit(solution)/shard_map/reduce_scatter | solution.py:258
  802.7 37.9 %copy-start.34 = (f32[1024]{0:T(1024)S(1)}, f32[1024]{0:T(1024)}, u32[]{:S(2)}) copy-start(f32[1024]{0:T(1024)} %get-tuple-element.224) | copy-start | bytes 12292
  802.7 37.9 %copy-start.36 = (f32[1024]{0:T(1024)S(1)}, f32[1024]{0:T(1024)}, u32[]{:S(2)}) copy-start(f32[1024]{0:T(1024)} %get-tuple-element.227) | copy-start | bytes 12292
  802.7 37.9 %copy-start.41 = (f32[1024]{0:T(1024)S(1)}, f32[1024]{0:T(1024)}, u32[]{:S(2)}) copy-start(f32[1024]{0:T(1024)} %get-tuple-element.228) | copy-start | bytes 12292
  802.7 249.2 %reduce-scatter.33.cloned.1.call-start = ((), (), s32[]{:S(2)}) async-start(), calls=%async_computation.22 | async-start | bytes 540672
  808.2 33.5 %copy-start.33 = (f32[1024]{0:T(1024)S(1)}, f32[1024]{0:T(1024)}, u32[]{:S(2)}) copy-start(f32[1024]{0:T(1024)} %get-tuple-element.219) | copy-start | bytes 12292
  808.2 33.5 %copy-start.35 = (f32[1024]{0:T(1024)S(1)}, f32[1024]{0:T(1024)}, u32[]{:S(2)}) copy-start(f32[1024]{0:T(1024)} %get-tuple-element.222) | copy-start | bytes 12292
  808.2 33.5 %copy-start.40 = (f32[1024]{0:T(1024)S(1)}, f32[1024]{0:T(1024)}, u32[]{:S(2)}) copy-start(f32[1024]{0:T(1024)} %get-tuple-element.215) | copy-start | bytes 12292
  841.6 342.0 %reduce-scatter.31.cloned.1.call-start = ((), (), s32[]{:S(2)}) async-start(), calls=%async_computation.21 | async-start | bytes 540672
  842.8 429.3 %reduce-scatter.29.cloned.1.call-start = ((), (), s32[]{:S(2)}) async-start(), calls=%async_computation.20 | async-start | bytes 4718592 | tf_op jit(solution)/shard_map/reduce_scatter | solution.py:261
  855.1 509.1 %reduce-scatter.27.cloned.1.call-start = ((), (), s32[]{:S(2)}) async-start(), calls=%async_computation.19 | async-start | bytes 4718592 | tf_op jit(solution)/shard_map/reduce_scatter | solution.py:260
  867.0 51.5 %copy-start.15 = (bf16[512,1024]{1,0:T(8,128)(2,1)S(1)}, bf16[512,1024]{1,0:T(8,128)(2,1)}, u32[]{:S(2)}) copy-start(bf16[512,1024]{1,0:T(8,128)(2,1)} %reduce-scatter.21.cloned.1.call-done) | copy-start | bytes 3145732
  867.0 564.8 %reduce-scatter.25.cloned.1.call-start = ((), (), s32[]{:S(2)}) async-start(), calls=%async_computation.18 | async-start | bytes 1179648 | tf_op jit(solution)/shard_map/reduce_scatter | solution.py:259
  872.7 559.1 %copy-start.1 = (bf16[1024,1024]{1,0:T(8,128)(2,1)S(1)}, bf16[1024,1024]{1,0:T(8,128)(2,1)}, u32[]{:S(2)}) copy-start(bf16[1024,1024]{1,0:T(8,128)(2,1)} %param.18) | copy-start | bytes 6291460
  (28 other events, 58.5 us)
Sparse Core Ops, SparseCore 0:
  104.3 74.3 reduce-scatter.14
  186.6 58.2 all-gather.3
  271.3 71.6 reduce-scatter.16
  354.1 34.4 all-gather.5
  409.8 71.7 reduce-scatter.18
  492.4 34.4 all-gather.7
  793.3 44.5 reduce-scatter.20
  841.5 75.0 reduce-scatter.22
  918.8 133.0 reduce-scatter.32
  1054.0 129.5 reduce-scatter.30
  1187.8 84.1 reduce-scatter.28
  1276.5 87.6 reduce-scatter.26
  1368.2 63.5 reduce-scatter.24
where the time goes:
time: 1450 us; the launch traced here: 1440 us
  waiting for transfers between devices  919 us (63%)
  matrix products  263 us (18%)
  other arithmetic  138 us (10%)
  local copies, waits for them, and re-layouts  89.2 us (6%)
  between operations  15 us (1%)
    unnamed x15, waiting for transfers between devices  260 us
    reduce_scatter x2, waiting for transfers between devices, branch_out(): lax.psum_scatter(partial_value, 'tensor', scatter_dimension=0, tiled=True)  139 us
    reduce_scatter x1, waiting for transfers between devices, per_device(): lax.psum_scatter(up_grad, 'dp', scatter_dimension=0, tiled=True)  92.2 us
    reduce_scatter x1, waiting for transfers between devices, per_device(): lax.psum_scatter(down_grad, 'dp', scatter_dimension=1, tiled=True)  87.1 us
    reduce_scatter x1, waiting for transfers between devices, per_device(): lax.psum_scatter(mid_partial, 'tensor', scatter_dimension=0, tiled=True)  71.7 us
    reduce_scatter x1, waiting for transfers between devices, per_device(): lax.psum_scatter(out_weight_grad, 'dp', scatter_dimension=1, tiled=True)  67.6 us
    all_gather x1, waiting for transfers between devices, per_device(): middle = lax.all_gather(state_rows, 'tensor', axis=0, tiled=True)  58.4 us
    dynamic_update_slice x8, local copies, waits for them, and re-layouts, attend_backward(): lax.scan(one_block, (zeros_seq, zeros_seq), jnp.arange(blocks, dtype=jnp....  46.5 us
  transfers between devices with their start and end apart: 13, of which 13 were waited for; matrix products, arithmetic and copies ran while one was open for 4% of the time, Pallas kernels for 0%

commit v1 on v0

v1 whole, which is shorter than its diff:
```python
import functools
import math

import jax
import jax.numpy as jnp
from jax import lax
from jax.experimental import pallas as pl
from jax.experimental.pallas import tpu as pltpu
from jax.sharding import PartitionSpec as P

DH = 64
SEQ = 2048
EPS = 1e-05
F32 = jnp.float32
BF16 = jnp.bfloat16
LANES = 128
NT = (((1,), (1,)), ((), ()))
TN = (((0,), (0,)), ((), ()))
VMEM_LIMIT = 56 * 2**20


def cost(micros, moved):
    return pl.CostEstimate(flops=int(micros * 1.1e9), bytes_accessed=moved, transcendentals=0)


def swap(field, axis, bit):
    size = lax.axis_size(axis)
    return lax.ppermute(field, axis, [(i, i ^ bit) for i in range(size)])


def core_swap(field):
    return swap(field, "tensor", 1)


def y_swap(field):
    return swap(field, "tensor", 2)


def pick(field, index, dim):
    return lax.dynamic_index_in_dim(field, index, dim, keepdims=False)


def halve(field, axis, bit, own, dim):
    sent = pick(field, 1 - own, dim).astype(BF16)
    kept = pick(field, own, dim).astype(F32)
    return kept + swap(sent, axis, bit).astype(F32)


def sum_over_dp(blocks, order):
    size = lax.axis_size("dp")
    index = lax.axis_index("dp")
    bits = [1 << k for k in range(size.bit_length() - 1)]
    todo = [bits[k] for k in order if k < len(bits)]
    todo += [b for b in bits if b not in todo]
    left = sorted(bits, reverse=True)
    tail = blocks.shape[1:]
    field = blocks
    for step, bit in enumerate(todo):
        place = left.index(bit)
        shape = (2 ** place, 2, 2 ** (len(left) - place - 1)) + tail
        own = (index // bit) % 2
        field = halve(field.reshape(shape), "dp", bit, own, 1)
        left.remove(bit)
        if step < len(todo) - 1:
            field = field.astype(BF16)
    return field.reshape(tail)


def fetch_from_y(shard):
    rows = shard.shape[0] // 4
    mine = lax.axis_index("dp") % 4
    got = y_swap(lax.dynamic_slice_in_dim(shard, mine * rows, rows, 0))
    one = swap(got, "dp", 1)
    two = swap(got, "dp", 2)
    half = rows // 2
    three_low = swap(two[:half], "dp", 1)
    three_high = swap(one[half:], "dp", 2)
    whole = jnp.zeros(shard.shape, shard.dtype)
    for piece, which in ((got, 0), (one, 1), (two, 2)):
        whole = lax.dynamic_update_slice_in_dim(whole, piece, (mine ^ which) * rows, 0)
    whole = lax.dynamic_update_slice_in_dim(whole, three_low, (mine ^ 3) * rows, 0)
    return lax.dynamic_update_slice_in_dim(whole, three_high, (mine ^ 3) * rows + half, 0)


def normalize(field):
    mean = jnp.mean(field, axis=-1, keepdims=True)
    centred = field - mean
    inverse = lax.rsqrt(jnp.mean(centred * centred, axis=-1, keepdims=True) + EPS)
    return centred * inverse, inverse


def norm_back(grad, unit, inverse, gain):
    scaled = grad * gain
    mean_one = jnp.mean(scaled, axis=-1, keepdims=True)
    mean_two = jnp.mean(scaled * unit, axis=-1, keepdims=True)
    return inverse * (scaled - mean_one - unit * mean_two)


def rotary_tables():
    half = DH // 2
    frequency = jnp.exp(jnp.arange(half, dtype=F32) * (-math.log(10000.0) / half))
    angles = jnp.arange(SEQ, dtype=F32)[:, None] * frequency[None, :]
    cosine, sine = jnp.cos(angles), jnp.sin(angles)
    return (
        jnp.concatenate([cosine] * 4, axis=1),
        jnp.concatenate([-sine, sine, -sine, sine], axis=1),
    )


def lanes_of(shape):
    return lax.broadcasted_iota(jnp.int32, shape, 1)


def partner_lanes(field):
    lane = lanes_of(field.shape)
    return jnp.where(lane % DH < DH // 2, pltpu.roll(field, 96, 1), pltpu.roll(field, 32, 1))


def rotate(field, cosine, sine):
    return field * cosine + partner_lanes(field) * sine


def rotate_back(field, cosine, sine):
    return field * cosine - partner_lanes(field) * sine


def split_three(field):
    high = field.astype(BF16).astype(F32)
    rest = field - high
    middle = rest.astype(BF16).astype(F32)
    return high, middle, rest - middle


def project_kernel(x_ref, w_ref, gain_ref, bias_ref, cos_ref, sin_ref, n_ref, q_ref, k_ref, v_ref):
    unit, unused = normalize(x_ref[...].astype(F32))
    normed = (unit * gain_ref[...] + bias_ref[...]).astype(BF16)
    n_ref[...] = normed
    rows = normed.shape[0]
    lane = lanes_of((rows, LANES))
    ones = jnp.where(lane < DH + 3, 1.0, 0.0)
    for which, out_ref in enumerate((q_ref, k_ref, v_ref)):
        both = jnp.dot(normed, w_ref[which], preferred_element_type=F32)
        for pair in range(both.shape[1] // LANES):
            field = both[:, pair * LANES : (pair + 1) * LANES]
            if which < 2:
                field = rotate(field, cos_ref[...], sin_ref[...])
            if which == 0:
                field = field * (1.0 / math.sqrt(DH))
            extra = jnp.zeros_like(field) if which == 0 else ones
            out_ref[2 * pair] = jnp.where(lane < DH, field, extra).astype(BF16)
            out_ref[2 * pair + 1] = jnp.where(lane < DH, pltpu.roll(field, DH, 1), extra).astype(BF16)


def project(inputs, w_qkv, gain, bias, cosine, sine):
    block = 256
    tokens, width = inputs.shape
    local = w_qkv.shape[2]
    heads = local // DH
    rows = lambda i: (i, 0)
    per_head = pl.BlockSpec((heads, block, LANES), lambda i: (0, i, 0))
    headed = jax.ShapeDtypeStruct((heads, tokens, LANES), BF16)
    return pl.pallas_call(
        project_kernel,
        grid=(tokens // block,),
        in_specs=[
            pl.BlockSpec((block, width), rows),
            pl.BlockSpec((3, width, local), lambda i: (0, 0, 0)),
            pl.BlockSpec((1, width), lambda i: (0, 0)),
            pl.BlockSpec((1, width), lambda i: (0, 0)),
            pl.BlockSpec((block, LANES), rows),
            pl.BlockSpec((block, LANES), rows),
        ],
        out_specs=[pl.BlockSpec((block, width), rows), per_head, per_head, per_head],
        out_shape=[jax.ShapeDtypeStruct((tokens, width), BF16), headed, headed, headed],
        compiler_params=pltpu.CompilerParams(vmem_limit_bytes=VMEM_LIMIT),
        cost_estimate=cost(8, 18 * 2**20),
        name="project",
    )(inputs, w_qkv, gain, bias, cosine, sine)


ROWS = 512
KEYS = 256


def attend_block(n, q_ref, k_ref, v_ref, out_ref, qa_ref):
    start, end = n * ROWS, (n + 1) * ROWS
    row = lax.broadcasted_iota(jnp.int32, (LANES, ROWS), 0)
    lane = lanes_of((ROWS, LANES))
    shape = (ROWS, ROWS)
    seen = lax.broadcasted_iota(jnp.int32, shape, 0) <= lax.broadcasted_iota(jnp.int32, shape, 1)
    outs = []
    for h in range(2):
        query = q_ref[h]
        last = lax.dot_general(k_ref[h, start:end, :], query, NT, preferred_element_type=F32)
        last = jnp.where(seen, last, -1e30)
        top = jnp.max(last, axis=0, keepdims=True)
        if n:
            scores = lax.dot_general(k_ref[h, :start, :], query, NT, preferred_element_type=F32)
            top = jnp.maximum(top, jnp.max(scores, axis=0, keepdims=True))
            early = jnp.exp(scores - top).astype(BF16)
        late = jnp.exp(last - top).astype(BF16)
        total = lax.dot_general(v_ref[h, start:end, :], late, TN, preferred_element_type=F32)
        if n:
            total = total + lax.dot_general(
                v_ref[h, :start, :], early, TN, preferred_element_type=F32
            )
        summed = total[DH : DH + 1, :]
        high, middle, low = split_three(-(top + jnp.log(summed)))
        extra = jnp.where(row == DH, high, jnp.where(row == DH + 1, middle, jnp.where(row == DH + 2, low, 0.0)))
        turned = jnp.transpose(jnp.where(row < DH, total * (1.0 / summed), extra))
        qa_ref[h] = jnp.where(lane < DH, query.astype(F32), turned).astype(BF16)
        outs.append(turned)
    out_ref[...] = jnp.where(lane < DH, outs[0], pltpu.roll(outs[1], DH, 1)).astype(BF16)


def attend_kernel(*refs):
    block = pl.program_id(1)
    for n in range(SEQ // ROWS):
        pl.when(block == n)(functools.partial(attend_block, n, *refs))


def attend(query, key_rows, value_rows):
    heads = query.shape[0]
    whole = pl.BlockSpec((2, SEQ, LANES), lambda p, i: (p, 0, 0))
    part = pl.BlockSpec((2, ROWS, LANES), lambda p, i: (p, i, 0))
    return pl.pallas_call(
        attend_kernel,
        grid=(heads // 2, SEQ // ROWS),
        in_specs=[part, whole, whole],
        out_specs=[pl.BlockSpec((ROWS, LANES), lambda p, i: (i, p)), part],
        out_shape=[
            jax.ShapeDtypeStruct((SEQ, heads * DH), BF16),
            jax.ShapeDtypeStruct((heads, SEQ, LANES), BF16),
        ],
        compiler_params=pltpu.CompilerParams(vmem_limit_bytes=VMEM_LIMIT),
        cost_estimate=cost(22, 9 * 2**20),
        name="attend",
    )(query, key_rows, value_rows)


def back_block(j, k_ref, v_ref, qa_ref, cos_ref, sin_ref, dk_ref, dv_ref, da_ref, dq_ref):
    start, length = j * KEYS, SEQ - j * KEYS
    rows = slice(start, start + KEYS)
    lane = lanes_of((KEYS, LANES))
    shape = (KEYS, KEYS)
    seen = lax.broadcasted_iota(jnp.int32, shape, 0) <= lax.broadcasted_iota(jnp.int32, shape, 1)
    key_grads, value_grads = [], []
    for h in range(2):
        keys, values = k_ref[h, rows, :], v_ref[h, rows, :]
        query, grad = qa_ref[h, start:, :], da_ref[h, start:, :]
        chance = jnp.exp(lax.dot_general(keys, query, NT, preferred_element_type=F32))
        first = jnp.where(seen, chance[:, :KEYS], 0.0)
        chance = jnp.concatenate([first, chance[:, KEYS:]], axis=1) if length > KEYS else first
        chance_grad = lax.dot_general(values, grad, NT, preferred_element_type=F32)
        score_grad = (chance * chance_grad).astype(BF16)
        value_grads.append(jnp.dot(chance.astype(BF16), grad, preferred_element_type=F32))
        key_grads.append(jnp.dot(score_grad, query, preferred_element_type=F32))
        turned = lax.dot_general(keys[:, :DH], score_grad, TN, preferred_element_type=F32)
        if j == 0:
            dq_ref[h] = turned
        else:
            dq_ref[h, :, start:] += turned
    key_grad = jnp.where(lane < DH, key_grads[0], pltpu.roll(key_grads[1], DH, 1))
    dk_ref[...] = rotate_back(key_grad, cos_ref[rows, :], sin_ref[rows, :]).astype(BF16)
    dv_ref[...] = jnp.where(lane < DH, value_grads[0], pltpu.roll(value_grads[1], DH, 1)).astype(BF16)


def back_kernel(
    k_ref, v_ref, qa_ref, grad_ref, out_ref, cos_ref, sin_ref, dq_ref, dk_ref, dv_ref, da_ref, turned_ref
):
    step = pl.program_id(1)
    steps = SEQ // KEYS

    @pl.when(step == 0)
    def _():
        def prepare(i, unused):
            rows = pl.ds(pl.multiple_of(i * KEYS, KEYS), KEYS)
            lane = lanes_of((KEYS, LANES))
            grad = grad_ref[rows, :].astype(F32)
            product = grad * out_ref[rows, :].astype(F32)
            for h in range(2):
                inner = jnp.sum(jnp.where(lane // DH == h, product, 0.0), axis=1, keepdims=True)
                high, middle, low = split_three(-inner)
                own = grad if h == 0 else pltpu.roll(grad, DH, 1)
                extra = jnp.where(lane == DH, high, jnp.where(lane == DH + 1, middle, jnp.where(lane == DH + 2, low, 0.0)))
                da_ref[h, rows, :] = jnp.where(lane < DH, own, extra).astype(BF16)
            return unused

        lax.fori_loop(0, steps, prepare, 0)

    for j in range(steps):
        pl.when(step == j)(
            functools.partial(
                back_block, j, k_ref, v_ref, qa_ref, cos_ref, sin_ref, dk_ref, dv_ref, da_ref, turned_ref
            )
        )

    @pl.when(step == steps - 1)
    def _():
        for i in range(steps):
            rows = slice(i * KEYS, (i + 1) * KEYS)
            both = jnp.concatenate([turned_ref[0, :, rows], turned_ref[1, :, rows]], axis=0)
            field = jnp.transpose(both) * (1.0 / math.sqrt(DH))
            dq_ref[rows, :] = rotate_back(field, cos_ref[rows, :], sin_ref[rows, :]).astype(BF16)


def attend_back(key_rows, value_rows, query_more, grad, out, cosine, sine):
    heads = key_rows.shape[0]
    whole = pl.BlockSpec((2, SEQ, LANES), lambda p, i: (p, 0, 0))
    pair = pl.BlockSpec((SEQ, LANES), lambda p, i: (0, p))
    table = pl.BlockSpec((SEQ, LANES), lambda p, i: (0, 0))
    part = pl.BlockSpec((KEYS, LANES), lambda p, i: (i, p))
    shape = jax.ShapeDtypeStruct((SEQ, heads * DH), BF16)
    return pl.pallas_call(
        back_kernel,
        grid=(heads // 2, SEQ // KEYS),
        in_specs=[whole, whole, whole, pair, pair, table, table],
        out_specs=[pair, part, part],
        out_shape=[shape, shape, shape],
        scratch_shapes=[pltpu.VMEM((2, SEQ, LANES), BF16), pltpu.VMEM((2, DH, SEQ), F32)],
        compiler_params=pltpu.CompilerParams(vmem_limit_bytes=VMEM_LIMIT),
        cost_estimate=cost(38, 13 * 2**20),
        name="attend_back",
    )(key_rows, value_rows, query_more, grad, out, cosine, sine)


def gelu_tanh(field):
    return jax.nn.gelu(field, approximate=True)


def product(left, right):
    return jnp.dot(left, right, preferred_element_type=F32)


def product_nt(left, right):
    return lax.dot_general(left, right, NT, preferred_element_type=F32)


def product_tn(left, right):
    return lax.dot_general(left, right, TN, preferred_element_type=F32)


def per_device(
    inputs, w_qkv, w_out, w_up, w_down, norm_gains, norm_biases, out_cot, group_ids, group_weights
):
    tokens, width = inputs.shape
    half, quarter = tokens // 2, tokens // 4
    place = lax.axis_index("tensor")
    y_own, core_own = place // 2, place % 2
    dp_size = lax.axis_size("dp")
    cosine, sine = rotary_tables()

    up_y = fetch_from_y(w_up)
    down_y = fetch_from_y(w_down)
    out_y = y_swap(w_out)
    outs = [w_out, out_y, core_swap(w_out), core_swap(out_y)]
    ups = [w_up, up_y, core_swap(w_up), core_swap(up_y)]
    downs = [w_down, down_y, core_swap(w_down), core_swap(down_y)]

    normed, query, key_rows, value_rows = project(
        inputs, w_qkv, norm_gains[0:1], norm_biases[0:1], cosine, sine
    )
    attended, query_more = attend(query, key_rows, value_rows)

    by_chip = attended.reshape(2, half, -1)
    mine = pick(by_chip, y_own, 0)
    theirs = y_swap(pick(by_chip, 1 - y_own, 0))
    chip_rows = jnp.concatenate([mine, theirs], axis=1)
    by_core = chip_rows.reshape(2, quarter, -1)
    row_parts = jnp.concatenate(
        [pick(by_core, core_own, 0), core_swap(pick(by_core, 1 - core_own, 0))], axis=1
    )

    branch = product(row_parts, jnp.concatenate(outs, axis=0))
    first_in = lax.dynamic_slice_in_dim(inputs, place * quarter, quarter, 0).astype(F32)
    attn_unit, attn_inverse = normalize(branch)
    middle = first_in + attn_unit * norm_gains[1] + norm_biases[1]
    mid_unit, mid_inverse = normalize(middle)
    mid_normed = (mid_unit * norm_gains[2] + norm_biases[2]).astype(BF16)
    hidden = [product(mid_normed, w) for w in ups]
    activated = [gelu_tanh(h).astype(BF16) for h in hidden]
    branch_two = sum(product(a, w) for a, w in zip(activated, downs))
    mlp_unit, mlp_inverse = normalize(branch_two)
    final_rows = middle + mlp_unit * norm_gains[3] + norm_biases[3]

    own_ids = lax.dynamic_slice_in_dim(group_ids, place * quarter, quarter, 0)
    groups = jnp.arange(group_weights.shape[0], dtype=jnp.int32)
    lookup = (own_ids[:, None] == groups[None, :]).astype(F32)
    row_weight = jnp.sum(lookup * group_weights[None, :], axis=1)
    own_cot = lax.dynamic_slice_in_dim(out_cot, place * quarter, quarter, 0)
    grad_out = own_cot.astype(F32) * row_weight[:, None]
    mlp_branch = norm_back(grad_out, mlp_unit, mlp_inverse, norm_gains[3]).astype(BF16)
    hidden_grad = []
    for h, w in zip(hidden, downs):
        unused, pullback = jax.vjp(gelu_tanh, h)
        hidden_grad.append(pullback(product_nt(mlp_branch, w))[0].astype(BF16))
    mid_grad = sum(product_nt(h, w) for h, w in zip(hidden_grad, ups))
    state_grad = grad_out + norm_back(mid_grad, mid_unit, mid_inverse, norm_gains[2])
    branch_grad = norm_back(state_grad, attn_unit, attn_inverse, norm_gains[1]).astype(BF16)

    sibling_branch = core_swap(branch_grad)
    chip_branch = jnp.where(
        core_own == 0,
        jnp.concatenate([branch_grad, sibling_branch], axis=0),
        jnp.concatenate([sibling_branch, branch_grad], axis=0),
    )
    attended_grad_y = y_swap(product_nt(chip_branch, outs[1]).astype(BF16))
    attended_grad_own = product_nt(chip_branch, outs[0]).astype(BF16)
    attended_grad = jnp.where(
        y_own == 0,
        jnp.concatenate([attended_grad_own, attended_grad_y], axis=0),
        jnp.concatenate([attended_grad_y, attended_grad_own], axis=0),
    )

    sibling_act = [core_swap(activated[2]), core_swap(activated[3])]
    sibling_mlp = core_swap(mlp_branch)
    sibling_hidden = [core_swap(hidden_grad[2]), core_swap(hidden_grad[3])]
    sibling_mid = core_swap(mid_normed)
    down_parts = [
        product_tn(activated[i], mlp_branch) + product_tn(sibling_act[i], sibling_mlp) for i in (0, 1)
    ]
    up_parts = [
        product_tn(mid_normed, hidden_grad[i]) + product_tn(sibling_mid, sibling_hidden[i]) for i in (0, 1)
    ]
    out_parts = [product_tn(rows, chip_branch) for rows in (mine, theirs)]

    def columns(field):
        return jnp.moveaxis(field.reshape(field.shape[0], dp_size, -1), 1, 0)

    def rows_of(field):
        return field.reshape((dp_size, -1) + field.shape[1:])

    def over_y(parts):
        return (parts[0] + y_swap(parts[1].astype(BF16)).astype(F32)).astype(BF16)

    down_total = sum_over_dp(columns(over_y(down_parts)), (0, 1, 2))
    up_total = sum_over_dp(rows_of(over_y(up_parts)), (0, 1, 2))
    out_total = sum_over_dp(columns(over_y(out_parts)), (0, 1, 2))

    query_grad, key_grad, value_grad = attend_back(
        key_rows, value_rows, query_more, attended_grad, attended, cosine, sine
    )
    proj_grad = jnp.concatenate([query_grad, key_grad, value_grad], axis=1)
    w_all = jnp.concatenate([w_qkv[0], w_qkv[1], w_qkv[2]], axis=1)
    in_partial = product_nt(proj_grad, w_all)
    qkv_grad = product_tn(normed, proj_grad).astype(BF16)
    qkv_total = sum_over_dp(rows_of(qkv_grad), (0, 1, 2))
    qkv_total = jnp.moveaxis(qkv_total.reshape(-1, 3, w_qkv.shape[2]), 1, 0)

    unit_all, inverse_all = normalize(inputs.astype(F32))
    gain_zero = jnp.sum(in_partial * unit_all, axis=0)
    bias_zero = jnp.sum(in_partial, axis=0)

    by_place = in_partial.reshape(2, 2, quarter, width)
    in_rows = halve(by_place, "tensor", 1, core_own, 1)
    in_rows = halve(in_rows, "tensor", 2, y_own, 0)
    unit_in, inverse_in = normalize(first_in)
    input_grad = state_grad + norm_back(in_rows, unit_in, inverse_in, norm_gains[0])

    def over_tokens(field):
        return jnp.sum(field, axis=0)

    sums = jnp.stack(
        [
            gain_zero,
            over_tokens(state_grad * attn_unit),
            over_tokens(mid_grad * mid_unit),
            over_tokens(grad_out * mlp_unit),
            bias_zero,
            over_tokens(state_grad),
            over_tokens(mid_grad),
            over_tokens(grad_out),
        ]
    )
    sums = lax.psum_scatter(sums, ("dp", "tensor"), scatter_dimension=1, tiled=True)
    return (
        final_rows.astype(BF16),
        input_grad,
        qkv_total,
        out_total,
        up_total,
        down_total,
        sums[:4],
        sums[4:],
    )


def solution(mesh):
    placed = (
        P("dp", None),
        P(None, None, "tensor"),
        P("tensor", None),
        P(None, "tensor"),
        P("tensor", None),
        P(),
        P(),
        P("dp", None),
        P("dp"),
        P(),
    )
    return jax.shard_map(
        per_device,
        mesh=mesh,
        in_specs=placed,
        out_specs=(
            P(("dp", "tensor"), None),
            P(("dp", "tensor"), None),
            P(None, "dp", "tensor"),
            P("tensor", "dp"),
            P("dp", "tensor"),
            P("tensor", "dp"),
            P(None, ("dp", "tensor")),
            P(None, ("dp", "tensor")),
        ),
        check_vma=False,
    )
```

time: 1450 us -> 496 us (0.34)
  waiting for transfers between devices: 919 us -> 202 us
  matrix products: 263 us -> 75.2 us
  other arithmetic: 138 us -> 53.8 us
  Pallas kernels: 0 us -> 72 us
  local copies, waits for them, and re-layouts: 89.2 us -> 35.8 us
  starting transfers between devices: 1.2 us -> 34.8 us
    reduce_scatter x8 -> x0, waiting for transfers between devices: 531 us -> none  [the longest x2 139 us: branch_out(): lax.psum_scatter(partial_value, 'tensor', scatter_dimension=0, tiled=True)]
    unnamed x15 -> x2, waiting for transfers between devices: 260 us -> 69.1 us
    dot_general x40 -> x31, matrix products: 263 us -> 75.2 us  [the longest x11 33.3 us: product_tn(): return lax.dot_general(left, right, TN, preferred_element_type=F32)]
    ppermute x0 -> x44, waiting for transfers between devices: none -> 132 us  [swap(): return lax.ppermute(field, axis, [(i, i ^ bit) for i in range(size)])]
    all_gather x3 -> x0, waiting for transfers between devices: 128 us -> none  [the longest x1 58.4 us: per_device(): middle = lax.all_gather(state_rows, 'tensor', axis=0, tiled=True)]
    pallas_call x0 -> x3, Pallas kernels: none -> 72 us  [the longest x1 38.1 us: attend_back(): pl.pallas_call(back_kernel, grid=(heads // 2, SEQ // KEYS), in_specs=[who...]
    dynamic_update_slice x8 -> x10, local copies, waits for them, and re-layouts: 46.5 us -> 0.35 us  [the longest x6 0.27 us: fetch_from_y(): lax.dynamic_update_slice_in_dim(whole, piece, (mine ^ which) * rows, 0)]
    reduce_sum x16 -> x10, other arithmetic: 51 us -> 15.7 us  [the longest x3 5.4 us: normalize(): mean = jnp.mean(field, axis=-1, keepdims=True)]
  transfers between devices with their start and end apart: 13 -> 45, of which waited for: 13 -> 17; matrix products, arithmetic and copies ran while one was open for 4% -> 32% of each run, Pallas kernels for 0% -> 15%
where the time goes in v1:
time: 496 us; the launch traced here: 489 us
  waiting for transfers between devices  202 us (41%)
  matrix products  75.2 us (15%)
  Pallas kernels  72 us (15%)
  other arithmetic  53.8 us (11%)
  local copies, waits for them, and re-layouts  35.8 us (7%)
  starting transfers between devices  34.8 us (7%)
  between operations  15.6 us (3%)
    ppermute x44, waiting for transfers between devices, swap(): return lax.ppermute(field, axis, [(i, i ^ bit) for i in range(size)])  132 us
    unnamed x2, waiting for transfers between devices  69.1 us
    pallas_call x1, Pallas kernels, attend_back(): pl.pallas_call(back_kernel, grid=(heads // 2, SEQ // KEYS), in_specs=[who...  38.1 us
    ppermute x44, starting transfers between devices, swap(): return lax.ppermute(field, axis, [(i, i ^ bit) for i in range(size)])  34.8 us
    dot_general x11, matrix products, product_tn(): return lax.dot_general(left, right, TN, preferred_element_type=F32)  33.3 us
    dot_general x11, matrix products, product_nt(): return lax.dot_general(left, right, NT, preferred_element_type=F32)  25 us
    pallas_call x1, Pallas kernels, attend(): pl.pallas_call(attend_kernel, grid=(heads // 2, SEQ // ROWS), in_specs=[p...  21.1 us
    dot_general x9, matrix products, product(): return jnp.dot(left, right, preferred_element_type=F32)  16.9 us
  transfers between devices with their start and end apart: 45, of which 17 were waited for; matrix products, arithmetic and copies ran while one was open for 32% of the time, Pallas kernels for 15%

profile of v1, /device:TPU:0, one launch (start us, length us, event | category | flops | bytes accessed | tf_op | source)
XLA Modules:
  0.0 488.7 jit_solution(5651174153481431724)
XLA Ops:
  7.2 3.0 collective-permute-start.2
  10.3 3.9 fusion.82
  14.8 3.0 pad_maximum_fusion
  17.8 12.9 %project.1 = (bf16[2048,1024]{1,0:T(8,128)(2,1)}, bf16[4,2048,128]{2,1,0:T(8,128)(2,1)}, bf16[4,2048,128]{2,1,0:T(8,128)(2,1)}, bf16[4,2048,128]{2,1,0:T(8,128)(2,1)}) custom-call(bf16[2048,1024]{1,0:T(8,128)(2,1)} %x_ref.1, bf16[3,1024,256]{2,1,0:T(8,128)(2,1)} %w_ref.1, f32[1,1024]{1,0:T(1,128)} %get-tuple-element.94.gain_ref, ...), custom_call_target="tpu_custom_call" | custom-call | flops 8800000000 | bytes 18874368 | tf_op jit(solution)/shard_map/project/pallas_call | solution.py:162
  30.7 21.1 %attend.1 = (bf16[2048,256]{1,0:T(8,128)(2,1)}, bf16[4,2048,128]{2,1,0:T(8,128)(2,1)}) custom-call(bf16[4,2048,128]{2,1,0:T(8,128)(2,1)} %get-tuple-element.17.refs_0_, bf16[4,2048,128]{2,1,0:T(8,128)(2,1)} %get-tuple-element.18.refs_1_.k_ref, bf16[4,2048,128]{2,1,0:T(8,128)(2,1)} %get-tuple-element.19.refs_2_.v_ref), custom_call_target="tpu_custom_call" | custom-call | flops 24199999488 | bytes 9437184 | tf_op jit(solution)/shard_map/attend/pallas_call | solution.py:226
  59.8 2.8 convert_reduce_fusion
  64.1 3.4 fusion.2
  71.8 8.3 %collective-permute-done.5 = bf16[256,1024]{1,0:T(8,128)(2,1)S(1)} collective-permute-done((bf16[256,1024]{1,0:T(8,128)(2,1)}, bf16[256,1024]{1,0:T(8,128)(2,1)S(1)}, u32[]{:S(2)}, u32[]{:S(2)}) %collective-permute-start.5) | collective-permute-done | bytes 524320 | tf_op jit(solution)/shard_map/ppermute | solution.py:28
  80.4 10.5 %collective-permute-done.10 = bf16[256,1024]{1,0:T(8,128)(2,1)S(1)} collective-permute-done((bf16[256,1024]{1,0:T(8,128)(2,1)}, bf16[256,1024]{1,0:T(8,128)(2,1)S(1)}, u32[]{:S(2)}, u32[]{:S(2)}) %collective-permute-start.10) | collective-permute-done | bytes 524320 | tf_op jit(solution)/shard_map/ppermute | solution.py:28
  95.3 2.7 fusion.98
  99.6 8.1 %collective-permute-done.7 = bf16[256,1024]{1,0:T(8,128)(2,1)S(1)} collective-permute-done((bf16[256,1024]{1,0:T(8,128)(2,1)S(1)}, bf16[256,1024]{1,0:T(8,128)(2,1)S(1)}, u32[]{:S(2)}, u32[]{:S(2)}) %collective-permute-start.7) | collective-permute-done | bytes 524320 | tf_op jit(solution)/shard_map/ppermute | solution.py:28
  113.8 5.1 %collective-permute-done.12 = bf16[256,1024]{1,0:T(8,128)(2,1)S(1)} collective-permute-done((bf16[256,1024]{1,0:T(8,128)(2,1)S(1)}, bf16[256,1024]{1,0:T(8,128)(2,1)S(1)}, u32[]{:S(2)}, u32[]{:S(2)}) %collective-permute-start.12) | collective-permute-done | bytes 524320 | tf_op jit(solution)/shard_map/ppermute | solution.py:28
  123.2 4.5 collective-permute-done.13
  131.9 2.9 multiply_convert_fusion.3
  136.5 3.1 multiply_convert_fusion.2
  144.9 2.4 fusion.27
  147.3 2.4 fusion.20
  154.7 2.4 fusion.41
  157.6 2.8 fusion.34
  164.8 2.3 multiply_reduce_fusion.2
  168.7 3.4 fusion.87
  173.5 3.2 fusion.105
  176.9 2.3 convolution_convert_fusion.2
  180.0 3.9 add_convert_fusion.1
  185.4 3.9 add_convert_fusion.3
  189.8 2.6 convolution_convert_fusion.1
  194.0 3.3 fusion.108
  197.3 3.3 fusion.106
  202.7 38.1 %attend_back.1 = (bf16[2048,256]{1,0:T(8,128)(2,1)}, bf16[2048,256]{1,0:T(8,128)(2,1)}, bf16[2048,256]{1,0:T(8,128)(2,1)}) custom-call(bf16[4,2048,128]{2,1,0:T(8,128)(2,1)} %get-tuple-element.18.refs_1_.k_ref, bf16[4,2048,128]{2,1,0:T(8,128)(2,1)} %get-tuple-element.19.refs_2_.v_ref, bf16[4,2048,128]{2,1,0:T(8,128)(2,1)} %get-tuple-element.21.qa_ref, ...), custom_call_target="tpu_custom_call" | custom-call | flops 41799999488 | bytes 13631488 | tf_op jit(solution)/shard_map/attend_back/pallas_call | solution.py:314
  243.9 6.0 %fusion.91 = (f32[1024]{0:T(1024)S(1)}, f32[1024]{0:T(1024)S(1)}, f32[2048,1024]{1,0:T(8,128)}) fusion(f32[2048]{0:T(1024)S(1)} %add_rsqrt_fusion, f32[2048]{0:T(1024)S(1)} %broadcast_multiply_fusion, bf16[2048,1024]{1,0:T(8,128)(2,1)S(1)} %copy-done, bf16[2048,768]{1,0:T(8,128)(2,1)S(1)} %constant_dynamic-update-slice_fusion.10, ...), kind=kOutput, calls=%fused_computation.218 | convolution fusion | flops 3238524928 | bytes 17326080 | tf_op jit(solution)/shard_map/dot_general | solution.py:336
  251.0 45.6 %collective-permute-done.26 = bf16[256,1024]{1,0:T(8,128)(2,1)} collective-permute-done((bf16[256,1024]{1,0:T(8,128)(2,1)}, bf16[256,1024]{1,0:T(8,128)(2,1)}, u32[]{:S(2)}, u32[]{:S(2)}) %collective-permute-start.26) | collective-permute-done | bytes 524320 | tf_op jit(solution)/shard_map/ppermute | solution.py:28
  296.6 3.1 fusion.66
  301.7 3.6 convolution_convert_fusion
  305.8 2.7 collective-permute-done.27
  308.6 2.2 collective-permute-start.28
  310.8 3.8 fusion.43
  314.7 3.0 collective-permute-start.29
  317.7 69.1 %reduce-scatter.4.cloned.1.call-done = f32[32,8]{1,0:T(8,128)} async-done(((f32[1024,8]{1,0:T(8,128)}), f32[32,8]{1,0:T(8,128)}) %reduce-scatter.4.cloned.1.call-update) | async-done | bytes 1040
  392.0 6.7 %add_convert_fusion = bf16[1024,1024]{0,1:T(8,128)(2,1)} fusion(bf16[1024,1024]{0,1:T(8,128)(2,1)} %collective-permute-done.40, f32[1024,1024]{0,1:T(8,128)} %fusion.87, f32[1024,1024]{0,1:T(8,128)} %fusion.108), kind=kLoop, calls=%fused_computation.9 | loop fusion | flops 4194304 | bytes 12582912 | tf_op jit(solution)/shard_map/convert_element_type | solution.py:434
  398.7 4.2 copy.50
  404.5 5.5 %add_convert_fusion.2 = bf16[1024,1024]{1,0:T(8,128)(2,1)S(1)} fusion(bf16[1024,1024]{1,0:T(8,128)(2,1)} %collective-permute-done.33, f32[1024,1024]{1,0:T(8,128)} %fusion.105, f32[1024,1024]{1,0:T(8,128)} %fusion.106), kind=kLoop, calls=%fused_computation.11 | loop fusion | flops 4194304 | bytes 12582912 | tf_op jit(solution)/shard_map/convert_element_type | solution.py:434
  412.2 2.3 bitcast_add_fusion
  415.7 14.8 %collective-permute-done.41 = bf16[4,1,1024,128]{3,2,0,1:T(8,128)(2,1)S(1)} collective-permute-done((bf16[4,1,1024,128]{3,2,0,1:T(8,128)(2,1)S(1)}, bf16[4,1,1024,128]{3,2,0,1:T(8,128)(2,1)S(1)}, u32[]{:S(2)}, u32[]{:S(2)}) %collective-permute-start.41) | collective-permute-done | bytes 1048608 | tf_op jit(solution)/shard_map/ppermute | solution.py:28
  433.8 14.3 %collective-permute-done.34 = bf16[4,1,128,1024]{3,2,0,1:T(8,128)(2,1)S(1)} collective-permute-done((bf16[4,1,128,1024]{3,2,0,1:T(8,128)(2,1)S(1)}, bf16[4,1,128,1024]{3,2,0,1:T(8,128)(2,1)S(1)}, u32[]{:S(2)}, u32[]{:S(2)}) %collective-permute-start.34) | collective-permute-done | bytes 1048608 | tf_op jit(solution)/shard_map/ppermute | solution.py:28
  456.6 6.6 %collective-permute-done.35 = bf16[2,1,128,1024]{3,2,0,1:T(8,128)(2,1)} collective-permute-done((bf16[2,1,128,1024]{3,2,0,1:T(8,128)(2,1)}, bf16[2,1,128,1024]{3,2,0,1:T(8,128)(2,1)}, u32[]{:S(2)}, u32[]{:S(2)}) %collective-permute-start.35) | collective-permute-done | bytes 524320 | tf_op jit(solution)/shard_map/ppermute | solution.py:28
  466.1 2.5 fusion.83
  471.1 5.7 %collective-permute-done.43 = bf16[1,1,1024,128]{3,2,0,1:T(8,128)(2,1)S(1)} collective-permute-done((bf16[1,1,1024,128]{3,2,0,1:T(8,128)(2,1)S(1)}, bf16[1,1,1024,128]{3,2,0,1:T(8,128)(2,1)S(1)}, u32[]{:S(2)}, u32[]{:S(2)}) %collective-permute-start.43) | collective-permute-done | bytes 262176 | tf_op jit(solution)/shard_map/ppermute | solution.py:28
  477.6 3.1 collective-permute-done.36
  (287 shorter events, 96.7 us)
Async XLA Ops:
  7.2 379.6 %reduce-scatter.4.cloned.1.call-start = ((), (), s32[]{:S(2)}) async-start(), calls=%async_computation.1 | async-start | bytes 540672
  7.2 62.9 %collective-permute-start.2 = (bf16[256,1024]{1,0:T(8,128)(2,1)}, bf16[256,1024]{1,0:T(8,128)(2,1)}, u32[]{:S(2)}, u32[]{:S(2)}) collective-permute-start(bf16[256,1024]{1,0:T(8,128)(2,1)} %param.12), channel_id=1, source_target_pairs={{0,2},{1,3},{2,0},{3,1},{4,6},{5,7},{6,4},{7,5},{8,10},{9,11},{10,... | collective-permute-start | bytes 1572872 | tf_op jit(solution)/shard_map/ppermute | solution.py:28
  10.3 82.4 %collective-permute-start.3 = (bf16[256,1024]{1,0:T(8,128)(2,1)}, bf16[256,1024]{1,0:T(8,128)(2,1)}, u32[]{:S(2)}, u32[]{:S(2)}) collective-permute-start(bf16[256,1024]{1,0:T(8,128)(2,1)} %param.12), channel_id=1, source_target_pairs={{0,1},{1,0},{2,3},{3,2},{4,5},{5,4},{6,7},{7,6},{8,9},{9,8},{10,11... | collective-permute-start | bytes 1572872 | tf_op jit(solution)/shard_map/ppermute | solution.py:28
  53.9 15.0 %collective-permute-start = (bf16[1024,256]{1,0:T(8,128)(2,1)}, bf16[1024,256]{1,0:T(8,128)(2,1)}, u32[]{:S(2)}, u32[]{:S(2)}) collective-permute-start(bf16[1024,256]{1,0:T(8,128)(2,1)} %get-tuple-element.88), channel_id=1, source_target_pairs={{0,2},{1,3},{2,0},{3,1},{4,6},{5,7},{6,4},{7,5},{8,10},{9,11},{10,... | collective-permute-start | bytes 1572872 | tf_op jit(solution)/shard_map/ppermute | solution.py:28
  55.9 24.1 %collective-permute-start.5 = (bf16[256,1024]{1,0:T(8,128)(2,1)}, bf16[256,1024]{1,0:T(8,128)(2,1)S(1)}, u32[]{:S(2)}, u32[]{:S(2)}) collective-permute-start(bf16[256,1024]{1,0:T(8,128)(2,1)} %constant_dynamic-slice_fusion.5), channel_id=1, source_target_pairs={{0,2},{1,3},{2,0},{3,1},{4,6},{5,7},{6,4},{7,5},{8,10},{9,11},{10,... | collective-permute-start | bytes 1572872 | tf_op jit(solution)/shard_map/ppermute | solution.py:28
  59.6 31.2 %collective-permute-start.10 = (bf16[256,1024]{1,0:T(8,128)(2,1)}, bf16[256,1024]{1,0:T(8,128)(2,1)S(1)}, u32[]{:S(2)}, u32[]{:S(2)}) collective-permute-start(bf16[256,1024]{1,0:T(8,128)(2,1)} %constant_dynamic-slice_fusion.4), channel_id=1, source_target_pairs={{0,2},{1,3},{2,0},{3,1},{4,6},{5,7},{6,4},{7,5},{8,10},{9,11},{10,... | collective-permute-start | bytes 1572872 | tf_op jit(solution)/shard_map/ppermute | solution.py:28
  70.0 24.3 %collective-permute-start.1 = (bf16[512,512]{1,0:T(8,128)(2,1)S(1)}, bf16[512,512]{1,0:T(8,128)(2,1)S(1)}, u32[]{:S(2)}, u32[]{:S(2)}) collective-permute-start(bf16[512,512]{1,0:T(8,128)(2,1)S(1)} %get-tuple-element.87), channel_id=1, source_target_pairs={{0,1},{1,0},{2,3},{3,2},{4,5},{5,4},{6,7},{7,6},{8,9},{9,8},{10,11... | collective-permute-start | bytes 1572872 | tf_op jit(solution)/shard_map/ppermute | solution.py:28
  70.1 24.7 %collective-permute-start.4 = (bf16[256,1024]{1,0:T(8,128)(2,1)}, bf16[256,1024]{1,0:T(8,128)(2,1)S(1)}, u32[]{:S(2)}, u32[]{:S(2)}) collective-permute-start(bf16[256,1024]{1,0:T(8,128)(2,1)} %collective-permute-done.2), channel_id=1, source_target_pairs={{0,1},{1,0},{2,3},{3,2},{4,5},{5,4},{6,7},{7,6},{8,9},{9,8},{10,11... | collective-permute-start | bytes 1572872 | tf_op jit(solution)/shard_map/ppermute | solution.py:28
  80.0 51.9 %collective-permute-start.15 = (bf16[1024,1024]{1,0:T(8,128)(2,1)S(1)}, bf16[1024,1024]{1,0:T(8,128)(2,1)S(1)}, u32[]{:S(2)}, u32[]{:S(2)}) collective-permute-start(bf16[1024,1024]{1,0:T(8,128)(2,1)S(1)} %copy-done.25), channel_id=1, source_target_pairs={{0,1},{1,0},{2,3},{3,2},{4,5},{5,4},{6,7},{7,6},{8,9},{9,8},{10,11... | collective-permute-start | bytes 6291464 | tf_op jit(solution)/shard_map/ppermute | solution.py:28
  90.9 17.7 %collective-permute-start.6 = (bf16[256,1024]{1,0:T(8,128)(2,1)S(1)}, bf16[256,1024]{1,0:T(8,128)(2,1)S(1)}, u32[]{:S(2)}, u32[]{:S(2)}) collective-permute-start(bf16[256,1024]{1,0:T(8,128)(2,1)S(1)} %collective-permute-done.5), channel_id=1, source_target_pairs={{0,4},{4,0},{8,12},{12,8},{16,20},{20,16},{24,28},{28,24},{1,5},{5... | collective-permute-start | bytes 1572872 | tf_op jit(solution)/shard_map/ppermute | solution.py:28
  92.7 14.9 %collective-permute-start.7 = (bf16[256,1024]{1,0:T(8,128)(2,1)S(1)}, bf16[256,1024]{1,0:T(8,128)(2,1)S(1)}, u32[]{:S(2)}, u32[]{:S(2)}) collective-permute-start(bf16[256,1024]{1,0:T(8,128)(2,1)S(1)} %collective-permute-done.5), channel_id=1, source_target_pairs={{0,8},{4,12},{8,0},{12,4},{16,24},{20,28},{24,16},{28,20},{1,9},{5... | collective-permute-start | bytes 1572872 | tf_op jit(solution)/shard_map/ppermute | solution.py:28
  94.3 24.5 %collective-permute-start.11 = (bf16[256,1024]{1,0:T(8,128)(2,1)S(1)}, bf16[256,1024]{1,0:T(8,128)(2,1)S(1)}, u32[]{:S(2)}, u32[]{:S(2)}) collective-permute-start(bf16[256,1024]{1,0:T(8,128)(2,1)S(1)} %collective-permute-done.10), channel_id=1, source_target_pairs={{0,4},{4,0},{8,12},{12,8},{16,20},{20,16},{24,28},{28,24},{1,5},{5... | collective-permute-start | bytes 1572872 | tf_op jit(solution)/shard_map/ppermute | solution.py:28
  94.9 24.0 %collective-permute-start.12 = (bf16[256,1024]{1,0:T(8,128)(2,1)S(1)}, bf16[256,1024]{1,0:T(8,128)(2,1)S(1)}, u32[]{:S(2)}, u32[]{:S(2)}) collective-permute-start(bf16[256,1024]{1,0:T(8,128)(2,1)S(1)} %collective-permute-done.10), channel_id=1, source_target_pairs={{0,8},{4,12},{8,0},{12,4},{16,24},{20,28},{24,16},{28,20},{1,9},{5... | collective-permute-start | bytes 1572872 | tf_op jit(solution)/shard_map/ppermute | solution.py:28
  107.6 13.6 %collective-permute-start.8 = (bf16[128,1024]{1,0:T(8,128)(2,1)S(1)}, bf16[128,1024]{1,0:T(8,128)(2,1)S(1)}, u32[]{:S(2)}, u32[]{:S(2)}) collective-permute-start(bf16[128,1024]{1,0:T(8,128)(2,1)S(1)} %slice.72), channel_id=1, source_target_pairs={{0,4},{4,0},{8,12},{12,8},{16,20},{20,16},{24,28},{28,24},{1,5},{5... | collective-permute-start | bytes 786440 | tf_op jit(solution)/shard_map/ppermute | solution.py:28
  108.6 14.4 %collective-permute-start.9 = (bf16[128,1024]{1,0:T(8,128)(2,1)S(1)}, bf16[128,1024]{1,0:T(8,128)(2,1)S(1)}, u32[]{:S(2)}, u32[]{:S(2)}) collective-permute-start(bf16[128,1024]{1,0:T(8,128)(2,1)S(1)} %slice.73), channel_id=1, source_target_pairs={{0,8},{4,12},{8,0},{12,4},{16,24},{20,28},{24,16},{28,20},{1,9},{5... | collective-permute-start | bytes 786440 | tf_op jit(solution)/shard_map/ppermute | solution.py:28
  118.9 16.0 %collective-permute-start.16 = (bf16[1024,1024]{1,0:T(8,128)(2,1)S(1)}, bf16[1024,1024]{1,0:T(8,128)(2,1)S(1)}, u32[]{:S(2)}, u32[]{:S(2)}) collective-permute-start(bf16[1024,1024]{1,0:T(8,128)(2,1)S(1)} %copy-done.24), channel_id=1, source_target_pairs={{0,1},{1,0},{2,3},{3,2},{4,5},{5,4},{6,7},{7,6},{8,9},{9,8},{10,11... | collective-permute-start | bytes 6291464 | tf_op jit(solution)/shard_map/ppermute | solution.py:28
  118.9 8.8 %collective-permute-start.13 = (bf16[128,1024]{1,0:T(8,128)(2,1)S(1)}, bf16[128,1024]{1,0:T(8,128)(2,1)S(1)}, u32[]{:S(2)}, u32[]{:S(2)}) collective-permute-start(bf16[128,1024]{1,0:T(8,128)(2,1)S(1)} %slice.74), channel_id=1, source_target_pairs={{0,4},{4,0},{8,12},{12,8},{16,20},{20,16},{24,28},{28,24},{1,5},{5... | collective-permute-start | bytes 786440 | tf_op jit(solution)/shard_map/ppermute | solution.py:28
  121.2 7.3 %collective-permute-start.14 = (bf16[128,1024]{1,0:T(8,128)(2,1)S(1)}, bf16[128,1024]{1,0:T(8,128)(2,1)S(1)}, u32[]{:S(2)}, u32[]{:S(2)}) collective-permute-start(bf16[128,1024]{1,0:T(8,128)(2,1)S(1)} %slice.75), channel_id=1, source_target_pairs={{0,8},{4,12},{8,0},{12,4},{16,24},{20,28},{24,16},{28,20},{1,9},{5... | collective-permute-start | bytes 786440 | tf_op jit(solution)/shard_map/ppermute | solution.py:28
  123.1 13.4 %collective-permute-start.17 = (bf16[1024,1024]{1,0:T(8,128)(2,1)S(1)}, bf16[1024,1024]{1,0:T(8,128)(2,1)S(1)}, u32[]{:S(2)}, u32[]{:S(2)}) collective-permute-start(bf16[1024,1024]{1,0:T(8,128)(2,1)S(1)} %constant_dynamic-update-slice_fusion.5), channel_id=1, source_target_pairs={{0,1},{1,0},{2,3},{3,2},{4,5},{5,4},{6,7},{7,6},{8,9},{9,8},{10,11... | collective-permute-start | bytes 6291464 | tf_op jit(solution)/shard_map/ppermute | solution.py:28
  127.7 56.2 %collective-permute-start.30 = (bf16[512,1024]{1,0:T(8,128)(2,1)S(1)}, bf16[512,1024]{1,0:T(8,128)(2,1)S(1)}, u32[]{:S(2)}, u32[]{:S(2)}) collective-permute-start(bf16[512,1024]{1,0:T(8,128)(2,1)S(1)} %add_convert_fusion.5), channel_id=1, source_target_pairs={{0,1},{1,0},{2,3},{3,2},{4,5},{5,4},{6,7},{7,6},{8,9},{9,8},{10,11... | collective-permute-start | bytes 3145736 | tf_op jit(solution)/shard_map/ppermute | solution.py:28
  128.5 11.1 %collective-permute-start.18 = (bf16[1024,1024]{1,0:T(8,128)(2,1)S(1)}, bf16[1024,1024]{1,0:T(8,128)(2,1)S(1)}, u32[]{:S(2)}, u32[]{:S(2)}) collective-permute-start(bf16[1024,1024]{1,0:T(8,128)(2,1)S(1)} %constant_dynamic-update-slice_fusion), channel_id=1, source_target_pairs={{0,1},{1,0},{2,3},{3,2},{4,5},{5,4},{6,7},{7,6},{8,9},{9,8},{10,11... | collective-permute-start | bytes 6291464 | tf_op jit(solution)/shard_map/ppermute | solution.py:28
  151.1 28.1 %collective-permute-start.38 = (bf16[512,1024]{1,0:T(8,128)(2,1)S(1)}, bf16[512,1024]{1,0:T(8,128)(2,1)S(1)}, u32[]{:S(2)}, u32[]{:S(2)}) collective-permute-start(bf16[512,1024]{1,0:T(8,128)(2,1)S(1)} %get-tuple-element.81), channel_id=1, source_target_pairs={{0,1},{1,0},{2,3},{3,2},{4,5},{5,4},{6,7},{7,6},{8,9},{9,8},{10,11... | collective-permute-start | bytes 3145736 | tf_op jit(solution)/shard_map/ppermute | solution.py:28
  151.7 27.7 %collective-permute-start.39 = (bf16[512,1024]{1,0:T(8,128)(2,1)S(1)}, bf16[512,1024]{1,0:T(8,128)(2,1)}, u32[]{:S(2)}, u32[]{:S(2)}) collective-permute-start(bf16[512,1024]{1,0:T(8,128)(2,1)S(1)} %get-tuple-element.105), channel_id=1, source_target_pairs={{0,1},{1,0},{2,3},{3,2},{4,5},{5,4},{6,7},{7,6},{8,9},{9,8},{10,11... | collective-permute-start | bytes 3145736 | tf_op jit(solution)/shard_map/ppermute | solution.py:28
  157.1 28.3 %collective-permute-start.32 = (bf16[512,1024]{1,0:T(8,128)(2,1)S(1)}, bf16[512,1024]{1,0:T(8,128)(2,1)}, u32[]{:S(2)}, u32[]{:S(2)}) collective-permute-start(bf16[512,1024]{1,0:T(8,128)(2,1)S(1)} %fusion.41), channel_id=1, source_target_pairs={{0,1},{1,0},{2,3},{3,2},{4,5},{5,4},{6,7},{7,6},{8,9},{9,8},{10,11... | collective-permute-start | bytes 3145736 | tf_op jit(solution)/shard_map/ppermute | solution.py:28
  167.8 8.9 %collective-permute-start.19 = (bf16[512,1024]{1,0:T(8,128)(2,1)S(1)}, bf16[512,1024]{1,0:T(8,128)(2,1)S(1)}, u32[]{:S(2)}, u32[]{:S(2)}) collective-permute-start(bf16[512,1024]{1,0:T(8,128)(2,1)S(1)} %multiply_convert_fusion), channel_id=1, source_target_pairs={{0,1},{1,0},{2,3},{3,2},{4,5},{5,4},{6,7},{7,6},{8,9},{9,8},{10,11... | collective-permute-start | bytes 3145736 | tf_op jit(solution)/shard_map/ppermute | solution.py:28
  176.7 15.8 %collective-permute-start.37 = (bf16[512,1024]{1,0:T(8,128)(2,1)S(1)}, bf16[512,1024]{1,0:T(8,128)(2,1)S(1)}, u32[]{:S(2)}, u32[]{:S(2)}) collective-permute-start(bf16[512,1024]{1,0:T(8,128)(2,1)S(1)} %copy-done.39), channel_id=1, source_target_pairs={{0,1},{1,0},{2,3},{3,2},{4,5},{5,4},{6,7},{7,6},{8,9},{9,8},{10,11... | collective-permute-start | bytes 3145736 | tf_op jit(solution)/shard_map/ppermute | solution.py:28
  179.2 18.1 %collective-permute-start.31 = (bf16[512,1024]{1,0:T(8,128)(2,1)S(1)}, bf16[512,1024]{1,0:T(8,128)(2,1)S(1)}, u32[]{:S(2)}, u32[]{:S(2)}) collective-permute-start(bf16[512,1024]{1,0:T(8,128)(2,1)S(1)} %copy-done.42), channel_id=1, source_target_pairs={{0,1},{1,0},{2,3},{3,2},{4,5},{5,4},{6,7},{7,6},{8,9},{9,8},{10,11... | collective-permute-start | bytes 3145736 | tf_op jit(solution)/shard_map/ppermute | solution.py:28
  179.5 22.0 %collective-permute-start.20 = (bf16[1024,256]{1,0:T(8,128)(2,1)S(1)}, bf16[1024,256]{1,0:T(8,128)(2,1)S(1)}, u32[]{:S(2)}, u32[]{:S(2)}) collective-permute-start(bf16[1024,256]{1,0:T(8,128)(2,1)S(1)} %convolution_convert_fusion.2), channel_id=1, source_target_pairs={{0,2},{1,3},{2,0},{3,1},{4,6},{5,7},{6,4},{7,5},{8,10},{9,11},{10,... | collective-permute-start | bytes 1572872 | tf_op jit(solution)/shard_map/ppermute | solution.py:28
  183.9 208.1 %collective-permute-start.40 = (bf16[1024,1024]{0,1:T(8,128)(2,1)}, bf16[1024,1024]{0,1:T(8,128)(2,1)}, u32[]{:S(2)}, u32[]{:S(2)}) collective-permute-start(bf16[1024,1024]{0,1:T(8,128)(2,1)} %add_convert_fusion.1), channel_id=1, source_target_pairs={{0,2},{1,3},{2,0},{3,1},{4,6},{5,7},{6,4},{7,5},{8,10},{9,11},{10,... | collective-permute-start | bytes 6291464 | tf_op jit(solution)/shard_map/ppermute | solution.py:28
  189.3 215.1 %collective-permute-start.33 = (bf16[1024,1024]{1,0:T(8,128)(2,1)}, bf16[1024,1024]{1,0:T(8,128)(2,1)}, u32[]{:S(2)}, u32[]{:S(2)}) collective-permute-start(bf16[1024,1024]{1,0:T(8,128)(2,1)} %add_convert_fusion.3), channel_id=1, source_target_pairs={{0,2},{1,3},{2,0},{3,1},{4,6},{5,7},{6,4},{7,5},{8,10},{9,11},{10,... | collective-permute-start | bytes 6291464 | tf_op jit(solution)/shard_map/ppermute | solution.py:28
  192.5 104.1 %collective-permute-start.26 = (bf16[256,1024]{1,0:T(8,128)(2,1)}, bf16[256,1024]{1,0:T(8,128)(2,1)}, u32[]{:S(2)}, u32[]{:S(2)}) collective-permute-start(bf16[256,1024]{1,0:T(8,128)(2,1)} %convolution_convert_fusion.1), channel_id=1, source_target_pairs={{0,2},{1,3},{2,0},{3,1},{4,6},{5,7},{6,4},{7,5},{8,10},{9,11},{10,... | collective-permute-start | bytes 1572872 | tf_op jit(solution)/shard_map/ppermute | solution.py:28
  243.9 52.7 %copy-start.9 = (bf16[1,1024,256]{2,1,0:T(8,128)(2,1)S(1)}, bf16[1,1024,256]{2,1,0:T(8,128)(2,1)}, u32[]{:S(2)}) copy-start(bf16[1,1024,256]{2,1,0:T(8,128)(2,1)} %copy-done.8) | copy-start | bytes 1572868
  251.0 50.8 %copy-start.23 = (bf16[2048,768]{1,0:T(8,128)(2,1)S(1)}, bf16[2048,768]{1,0:T(8,128)(2,1)}, u32[]{:S(2)}) copy-start(bf16[2048,768]{1,0:T(8,128)(2,1)} %copy-done.22) | copy-start | bytes 9437188
  251.0 50.8 %copy-start.49 = (bf16[2048,1024]{1,0:T(8,128)(2,1)S(1)}, bf16[2048,1024]{1,0:T(8,128)(2,1)}, u32[]{:S(2)}) copy-start(bf16[2048,1024]{1,0:T(8,128)(2,1)} %get-tuple-element.25) | copy-start | bytes 12582916
  299.9 8.6 %collective-permute-start.27 = (bf16[4,1,256,128]{3,2,0,1:T(8,128)(2,1)S(1)}, bf16[4,1,256,128]{3,2,0,1:T(8,128)(2,1)S(1)}, u32[]{:S(2)}, u32[]{:S(2)}) collective-permute-start(bf16[4,1,256,128]{3,2,0,1:T(8,128)(2,1)S(1)} %dynamic-slice_bitcast_fusion.7), channel_id=1, source_target_pairs={{0,4},{4,0},{8,12},{12,8},{16,20},{20,16},{24,28},{28,24},{1,5},{5... | collective-permute-start | bytes 786440 | tf_op jit(solution)/shard_map/ppermute | solution.py:28
  305.5 84.2 %collective-permute-start.23 = (bf16[4,1,128,768]{3,2,0,1:T(8,128)(2,1)S(1)}, bf16[4,1,128,768]{3,2,0,1:T(8,128)(2,1)}, u32[]{:S(2)}, u32[]{:S(2)}) collective-permute-start(bf16[4,1,128,768]{3,2,0,1:T(8,128)(2,1)S(1)} %dynamic-slice_bitcast_fusion.2), channel_id=1, source_target_pairs={{0,4},{4,0},{8,12},{12,8},{16,20},{20,16},{24,28},{28,24},{1,5},{5... | collective-permute-start | bytes 2359304 | tf_op jit(solution)/shard_map/ppermute | solution.py:28
  308.6 6.0 %collective-permute-start.28 = (bf16[2,1,256,128]{3,2,0,1:T(8,128)(2,1)S(1)}, bf16[2,1,256,128]{3,2,0,1:T(8,128)(2,1)S(1)}, u32[]{:S(2)}, u32[]{:S(2)}) collective-permute-start(bf16[2,1,256,128]{3,2,0,1:T(8,128)(2,1)S(1)} %dynamic-slice_bitcast_fusion.8), channel_id=1, source_target_pairs={{0,8},{4,12},{8,0},{12,4},{16,24},{20,28},{24,16},{28,20},{1,9},{5... | collective-permute-start | bytes 393224 | tf_op jit(solution)/shard_map/ppermute | solution.py:28
  314.7 97.5 %collective-permute-start.21 = (bf16[2,512,1024]{2,1,0:T(8,128)(2,1)}, bf16[2,512,1024]{2,1,0:T(8,128)(2,1)}, u32[]{:S(2)}, u32[]{:S(2)}) collective-permute-start(bf16[2,512,1024]{2,1,0:T(8,128)(2,1)} %fusion.43), channel_id=1, source_target_pairs={{0,1},{1,0},{2,3},{3,2},{4,5},{5,4},{6,7},{7,6},{8,9},{9,8},{10,11... | collective-permute-start | bytes 6291464 | tf_op jit(solution)/shard_map/ppermute | solution.py:28
  314.7 74.3 %collective-permute-start.29 = (bf16[1,1,256,128]{3,2,0,1:T(8,128)(2,1)S(1)}, bf16[1,1,256,128]{3,2,0,1:T(8,128)(2,1)S(1)}, u32[]{:S(2)}, u32[]{:S(2)}) collective-permute-start(bf16[1,1,256,128]{3,2,0,1:T(8,128)(2,1)S(1)} %constant_dynamic-slice_fusion.2), channel_id=1, source_target_pairs={{0,16},{4,20},{8,24},{12,28},{16,0},{20,4},{24,8},{28,12},{1,17},{... | collective-permute-start | bytes 196616 | tf_op jit(solution)/shard_map/ppermute | solution.py:28
  392.0 20.0 %collective-permute-start.24 = (bf16[2,1,128,768]{3,2,0,1:T(8,128)(2,1)}, bf16[2,1,128,768]{3,2,0,1:T(8,128)(2,1)S(1)}, u32[]{:S(2)}, u32[]{:S(2)}) collective-permute-start(bf16[2,1,128,768]{3,2,0,1:T(8,128)(2,1)} %dynamic-slice_bitcast_fusion.6), channel_id=1, source_target_pairs={{0,8},{4,12},{8,0},{12,4},{16,24},{20,28},{24,16},{28,20},{1,9},{5... | collective-permute-start | bytes 1179656 | tf_op jit(solution)/shard_map/ppermute | solution.py:28
  404.4 26.2 %collective-permute-start.41 = (bf16[4,1,1024,128]{3,2,0,1:T(8,128)(2,1)S(1)}, bf16[4,1,1024,128]{3,2,0,1:T(8,128)(2,1)S(1)}, u32[]{:S(2)}, u32[]{:S(2)}) collective-permute-start(bf16[4,1,1024,128]{3,2,0,1:T(8,128)(2,1)S(1)} %dynamic-slice_bitcast_fusion), channel_id=1, source_target_pairs={{0,4},{4,0},{8,12},{12,8},{16,20},{20,16},{24,28},{28,24},{1,5},{5... | collective-permute-start | bytes 3145736 | tf_op jit(solution)/shard_map/ppermute | solution.py:28
  410.1 38.1 %collective-permute-start.34 = (bf16[4,1,128,1024]{3,2,0,1:T(8,128)(2,1)S(1)}, bf16[4,1,128,1024]{3,2,0,1:T(8,128)(2,1)S(1)}, u32[]{:S(2)}, u32[]{:S(2)}) collective-permute-start(bf16[4,1,128,1024]{3,2,0,1:T(8,128)(2,1)S(1)} %dynamic-slice_bitcast_fusion.1), channel_id=1, source_target_pairs={{0,4},{4,0},{8,12},{12,8},{16,20},{20,16},{24,28},{28,24},{1,5},{5... | collective-permute-start | bytes 3145736 | tf_op jit(solution)/shard_map/ppermute | solution.py:28
  412.1 40.0 %collective-permute-start.25 = (bf16[1,1,128,768]{3,2,0,1:T(8,128)(2,1)S(1)}, bf16[1,1,128,768]{3,2,0,1:T(8,128)(2,1)S(1)}, u32[]{:S(2)}, u32[]{:S(2)}) collective-permute-start(bf16[1,1,128,768]{3,2,0,1:T(8,128)(2,1)S(1)} %constant_dynamic-slice_fusion.3), channel_id=1, source_target_pairs={{0,16},{4,20},{8,24},{12,28},{16,0},{20,4},{24,8},{28,12},{1,17},{... | collective-permute-start | bytes 589832 | tf_op jit(solution)/shard_map/ppermute | solution.py:28
  415.7 50.4 %collective-permute-start.22 = (bf16[512,1024]{1,0:T(8,128)(2,1)}, bf16[512,1024]{1,0:T(8,128)(2,1)S(1)}, u32[]{:S(2)}, u32[]{:S(2)}) collective-permute-start(bf16[512,1024]{1,0:T(8,128)(2,1)} %fusion.67), channel_id=1, source_target_pairs={{0,2},{1,3},{2,0},{3,1},{4,6},{5,7},{6,4},{7,5},{8,10},{9,11},{10,... | collective-permute-start | bytes 3145736 | tf_op jit(solution)/shard_map/ppermute | solution.py:28
  431.8 23.3 %collective-permute-start.42 = (bf16[2,1,1024,128]{3,2,0,1:T(8,128)(2,1)}, bf16[2,1,1024,128]{3,2,0,1:T(8,128)(2,1)}, u32[]{:S(2)}, u32[]{:S(2)}) collective-permute-start(bf16[2,1,1024,128]{3,2,0,1:T(8,128)(2,1)} %dynamic-slice_bitcast_fusion.3), channel_id=1, source_target_pairs={{0,8},{4,12},{8,0},{12,4},{16,24},{20,28},{24,16},{28,20},{1,9},{5... | collective-permute-start | bytes 1572872 | tf_op jit(solution)/shard_map/ppermute | solution.py:28
  450.4 12.8 %collective-permute-start.35 = (bf16[2,1,128,1024]{3,2,0,1:T(8,128)(2,1)}, bf16[2,1,128,1024]{3,2,0,1:T(8,128)(2,1)}, u32[]{:S(2)}, u32[]{:S(2)}) collective-permute-start(bf16[2,1,128,1024]{3,2,0,1:T(8,128)(2,1)} %dynamic-slice_bitcast_fusion.4), channel_id=1, source_target_pairs={{0,8},{4,12},{8,0},{12,4},{16,24},{20,28},{24,16},{28,20},{1,9},{5... | collective-permute-start | bytes 1572872 | tf_op jit(solution)/shard_map/ppermute | solution.py:28
  456.6 20.2 %collective-permute-start.43 = (bf16[1,1,1024,128]{3,2,0,1:T(8,128)(2,1)S(1)}, bf16[1,1,1024,128]{3,2,0,1:T(8,128)(2,1)S(1)}, u32[]{:S(2)}, u32[]{:S(2)}) collective-permute-start(bf16[1,1,1024,128]{3,2,0,1:T(8,128)(2,1)S(1)} %constant_dynamic-slice_fusion), channel_id=1, source_target_pairs={{0,16},{4,20},{8,24},{12,28},{16,0},{20,4},{24,8},{28,12},{1,17},{... | collective-permute-start | bytes 786440 | tf_op jit(solution)/shard_map/ppermute | solution.py:28
  464.7 16.1 %collective-permute-start.36 = (bf16[1,1,128,1024]{3,2,0,1:T(8,128)(2,1)S(1)}, bf16[1,1,128,1024]{3,2,0,1:T(8,128)(2,1)S(1)}, u32[]{:S(2)}, u32[]{:S(2)}) collective-permute-start(bf16[1,1,128,1024]{3,2,0,1:T(8,128)(2,1)S(1)} %constant_dynamic-slice_fusion.1), channel_id=1, source_target_pairs={{0,16},{4,20},{8,24},{12,28},{16,0},{20,4},{24,8},{28,12},{1,17},{... | collective-permute-start | bytes 786440 | tf_op jit(solution)/shard_map/ppermute | solution.py:28
  (51 other events, 387.3 us)
Sparse Core Ops, SparseCore 0:
  251.1 135.6 reduce-scatter.3
